TPU v7x, 32 devices: a whole 2x2x4 slice. The times are simulated.
32 devices in a mesh: clip: 8 (over z, x), seg: 4 (over y, core).
Axes of the slice: x: 2, y: 2, z: 4, core: 2. Of those that a mesh axis runs over, the one named last changes fastest.
Arguments:
- frames: bfloat16 [32, 4, 5, 48, 48, 3], P('clip', 'seg'), may hold values from -6 to 6
- features: bfloat16 [32, 4, 8, 8, 2048], P('clip', 'seg'), may hold values from -6 to 6
- res_group: int32 [32], replicated, may hold values from 0 to 2
- stem_weight: bfloat16 [7, 7, 3, 64], replicated, may hold values from -0.5 to 0.5
- diff_weight: bfloat16 [3, 3, 12, 64], replicated, may hold values from -1.75 to 1.75
- stem_gain: float32 [64], replicated, may hold values from 0.1 to 1.9
- stem_bias: float32 [64], replicated, may hold values from -0.5 to 0.5
- w_reduce: bfloat16 [2048, 512], replicated, may hold values from -0.125 to 0.125
- gain_one: float32 [512], replicated, may hold values from 0.1 to 1.9
- bias_one: float32 [512], replicated, may hold values from -0.5 to 0.5
- w_spatial: bfloat16 [3, 3, 512, 512], replicated, may hold values from -0.09375 to 0.09375
- gain_two: float32 [512], replicated, may hold values from 0.1 to 1.9
- bias_two: float32 [512], replicated, may hold values from -0.5 to 0.5
- w_expand: bfloat16 [512, 2048], replicated, may hold values from -0.25 to 0.25
- gain_three: float32 [2048], replicated, may hold values from 0.1 to 1.9
- bias_three: float32 [2048], replicated, may hold values from -0.5 to 0.5
- w_squeeze: bfloat16 [2048, 128], replicated, may hold values from -0.125 to 0.125
- w_fine: bfloat16 [3, 3, 128, 128], replicated, may hold values from -0.1875 to 0.1875
- w_coarse: bfloat16 [3, 3, 128, 128], replicated, may hold values from -0.1875 to 0.1875
- w_excite: bfloat16 [128, 2048], replicated, may hold values from -0.25 to 0.25
- stem_cotangent: bfloat16 [32, 4, 24, 24, 64], P('clip', 'seg'), may hold values from -6 to 6
- block_cotangent: bfloat16 [32, 4, 8, 8, 2048], P('clip', 'seg'), may hold values from -6 to 6
Outputs:
- stem_out: bfloat16 [32, 4, 24, 24, 64], P('clip', 'seg')
- block_out: bfloat16 [32, 4, 8, 8, 2048], P('clip', 'seg')
- grad_features: bfloat16 [32, 4, 8, 8, 2048], P('clip', 'seg')
- grad_stem_weight: float32 [7, 7, 3, 64], replicated
- grad_diff_weight: float32 [3, 3, 12, 64], replicated
- grad_stem_gain: float32 [64], replicated
- grad_stem_bias: float32 [64], replicated
- grad_w_reduce: float32 [2048, 512], replicated
- grad_gain_one: float32 [512], replicated
- grad_bias_one: float32 [512], replicated
- grad_w_spatial: float32 [3, 3, 512, 512], replicated
- grad_gain_two: float32 [512], replicated
- grad_bias_two: float32 [512], replicated
- grad_w_expand: float32 [512, 2048], replicated
- grad_gain_three: float32 [2048], replicated
- grad_bias_three: float32 [2048], replicated
- grad_w_squeeze: float32 [2048, 128], replicated
- grad_w_fine: float32 [3, 3, 128, 128], replicated
- grad_w_coarse: float32 [3, 3, 128, 128], replicated
- grad_w_excite: float32 [128, 2048], replicated
Inputs may be any that keep to these rules, and one draw needn't show every extreme that they name: `res_group`: groups 0, 1, 2 have valid feature grids of 5, 7, 8 cells on a side, placed at the grid's first rows and columns.
All inputs are finite; a program needn't handle non-finite values.
Results may differ from a plain program's by a relative error of at most 0.015.
Values may be sent and summed in bfloat16 or wider, within the bound.
A program may use at most 192 MiB of HBM per device.

v0:
```python
from functools import partial

import jax
import jax.numpy as jnp
from jax import lax
from jax.sharding import PartitionSpec as P


def with_halo(cells, sides, width):
    for axis, dim in sides:
        count = lax.axis_size(axis)
        ends = count - 1
        head = lax.slice_in_dim(cells, 0, width, axis=dim)
        tail = lax.slice_in_dim(cells, cells.shape[dim] - width, cells.shape[dim], axis=dim)
        cells = jnp.concatenate(
            [
                lax.ppermute(tail, axis, [(i, (i + 1) % count) for i in range(ends)]),
                cells,
                lax.ppermute(head, axis, [((i + 1) % count, i) for i in range(ends)]),
            ],
            axis=dim,
        )
    return cells


def for_sending(shard):

    def short(part):
        return part.astype(jnp.bfloat16) if part.dtype == jnp.float32 else part

    return jax.tree.map(short, shard)


def narrow(values):
    rounded = lax.optimization_barrier(values.astype(jnp.bfloat16)).astype(jnp.float32)
    return values + lax.stop_gradient(rounded - values)


def grad_round(values):
    return values.astype(jnp.bfloat16).astype(jnp.float32)


def silu_act(values):
    return values * jax.nn.sigmoid(values)


def convolve(image, kernel, stride):
    return lax.conv_general_dilated(
        image, kernel, (stride, stride), "SAME", dimension_numbers=("NHWC", "HWIO", "NHWC")
    )


def project(values, weight):
    return jnp.einsum("abcdk,kn->abcdn", values, weight)


def block_pool(image, factor):
    total, height, breadth, chans = image.shape
    return jnp.mean(
        image.reshape(total, height // factor, factor, breadth // factor, factor, chans),
        axis=(2, 4),
    )


def upsample(image):
    return jnp.repeat(jnp.repeat(image, 2, axis=1), 2, axis=2)


def local_moments(values, mask):
    axes = tuple(range(values.ndim - 1))
    weighted = values * mask
    return (jnp.sum(weighted, axis=axes), jnp.sum(weighted * values, axis=axes))


def normalize(values, sums, count, gain, bias):
    mean = sums[0] / count
    spread = sums[1] / count - mean * mean
    return (values - mean) * lax.rsqrt(spread + 1e-05) * gain + bias


def spatial(values, weight):
    lead = values.shape
    flat = values.reshape(lead[0] * lead[1], lead[2], lead[3], lead[4])
    return convolve(flat, weight, 1).reshape(lead[0], lead[1], lead[2], lead[3], weight.shape[3])


def multi_scale(diff, w_fine, w_coarse):
    lead = diff.shape
    flat = diff.reshape(lead[0] * lead[1], lead[2], lead[3], lead[4])
    fine = convolve(flat, w_fine, 1)
    coarse = upsample(convolve(narrow(block_pool(flat, 2)), w_coarse, 1))
    return (fine + coarse).reshape(lead)


def make_mask(groups, grid):
    side = 5 + 2 * groups - groups // 2
    cells = jnp.arange(grid, dtype=jnp.int32)
    inside = (cells[None, :] < side[:, None]).astype(jnp.float32)
    return inside[:, None, :, None, None] * inside[:, None, None, :, None]


def synced(values, mask):
    local_sums, pull_sums = jax.vjp(lambda inner: local_moments(inner, mask), values)
    return (lax.psum(local_sums, ("clip", "seg")), pull_sums)


def synced_back(grad_sums, pull_sums):
    return pull_sums(lax.psum(grad_sums, ("clip", "seg")))[0]


def stem_front(frames, stem_weight, diff_weight):
    images = frames.shape[0] * frames.shape[1]
    side = frames.shape[3]
    centre = frames[:, :, 2].reshape(images, side, side, 3)
    diffs = jnp.moveaxis(frames[:, :, 1:] - frames[:, :, :-1], 2, 4).reshape(images, side, side, 12)
    pooled = narrow(block_pool(diffs, 4))
    motion = upsample(convolve(pooled, diff_weight, 1))
    return convolve(centre, stem_weight, 2) + motion


def stem_rear(pre, sums, gain, bias, count, layout):
    return silu_act(normalize(pre, sums, count, gain, bias)).reshape(layout)


def piece_one(inputs, weight):
    return project(inputs, weight)


def piece_mid(values, sums, gain, bias, weight, mask, count, mixer):
    hidden = narrow(silu_act(normalize(values, sums, count, gain, bias)) * mask)
    return mixer(hidden, weight)


def piece_four(values, sums, gain, bias, weight, mask, count):
    branch = normalize(values, sums, count, gain, bias) * mask
    return (branch, narrow(project(narrow(branch), weight)))


def piece_five(inputs, branch, extended, w_fine, w_coarse, w_excite, mask):
    centre = extended[:, 1:2]
    motion = multi_scale(narrow(extended[:, 2:3] - centre), w_fine, w_coarse) + multi_scale(
        narrow(extended[:, 0:1] - centre), w_fine, w_coarse
    )
    gate = jax.nn.sigmoid(project(narrow(motion), w_excite))
    return silu_act(inputs + branch * (1.0 + gate)) * mask


def deep_forward(inputs, mask, count, deep):
    (
        reduce_w,
        g_one,
        b_one,
        spatial_w,
        g_two,
        b_two,
        expand_w,
        g_three,
        b_three,
        squeeze_w,
        fine_w,
        coarse_w,
        excite_w,
    ) = deep
    first, pull_one = jax.vjp(piece_one, inputs, reduce_w)
    sums_one, back_one = synced(first, mask)
    second, pull_two = jax.vjp(
        partial(piece_mid, mask=mask, count=count, mixer=spatial),
        first,
        sums_one,
        g_one,
        b_one,
        spatial_w,
    )
    sums_two, back_two = synced(second, mask)
    third, pull_three = jax.vjp(
        partial(piece_mid, mask=mask, count=count, mixer=project),
        second,
        sums_two,
        g_two,
        b_two,
        expand_w,
    )
    sums_three, back_three = synced(third, mask)
    (branch, squeezed), pull_four = jax.vjp(
        partial(piece_four, mask=mask, count=count), third, sums_three, g_three, b_three, squeeze_w
    )
    extended = with_halo(squeezed.astype(jnp.bfloat16), (("seg", 1),), 1).astype(jnp.float32)
    result, pull_five = jax.vjp(
        partial(piece_five, mask=mask), inputs, branch, extended, fine_w, coarse_w, excite_w
    )
    return (
        result,
        (pull_one, back_one, pull_two, back_two, pull_three, back_three, pull_four, pull_five),
    )


def deep_backward(grad_out, pulls):
    pull_one, back_one, pull_two, back_two, pull_three, back_three, pull_four, pull_five = pulls
    g_inputs, g_branch, g_ext, g_fine, g_coarse, g_excite = pull_five(grad_out)
    rims = with_halo(
        for_sending(jnp.concatenate([g_ext[:, 0:1], g_ext[:, 2:3]], axis=1)), (("seg", 1),), 1
    )
    g_squeezed = g_ext[:, 1:2] + rims[:, 0:1] + rims[:, 3:4]
    g_third, g_sums, g_g3, g_b3, g_squeeze = pull_four((g_branch, g_squeezed))
    g_third = grad_round(g_third + synced_back(g_sums, back_three))
    g_second, g_sums, g_g2, g_b2, g_expand = pull_three(g_third)
    g_second = grad_round(g_second + synced_back(g_sums, back_two))
    g_first, g_sums, g_g1, g_b1, g_spatial = pull_two(g_second)
    g_first = grad_round(g_first + synced_back(g_sums, back_one))
    g_more, g_reduce = pull_one(g_first)
    return (
        g_inputs + g_more,
        [
            g_reduce,
            g_g1,
            g_b1,
            g_spatial,
            g_g2,
            g_b2,
            g_expand,
            g_g3,
            g_b3,
            g_squeeze,
            g_fine,
            g_coarse,
            g_excite,
        ],
    )


def pack_grads(grads, parts):
    flat = jnp.concatenate([grad.reshape(-1) for grad in grads])
    stride = parts * 128
    padded = -(-flat.shape[0] // stride) * stride
    return jnp.pad(flat, (0, padded - flat.shape[0])).reshape(padded // 128, 128)


def unpack_grads(packed, grads):
    flat = packed.reshape(-1)
    pieces = []
    offset = 0
    for grad in grads:
        pieces.append(flat[offset : offset + grad.size].reshape(grad.shape))
        offset = offset + grad.size
    return pieces


def shards(
    frames,
    features,
    res_group,
    stem_weight,
    diff_weight,
    stem_gain,
    stem_bias,
    w_reduce,
    gain_one,
    bias_one,
    w_spatial,
    gain_two,
    bias_two,
    w_expand,
    gain_three,
    bias_three,
    w_squeeze,
    w_fine,
    w_coarse,
    w_excite,
    stem_cotangent,
    block_cotangent,
):
    parts = lax.axis_size("clip") * lax.axis_size("seg")
    local_clips = features.shape[0]
    groups = lax.dynamic_slice_in_dim(res_group, lax.axis_index("clip") * local_clips, local_clips)
    mask = make_mask(groups, features.shape[2])
    count = jnp.sum(make_mask(res_group, features.shape[2])) * lax.axis_size("seg")
    frames32 = frames.astype(jnp.float32)
    stem_w = stem_weight.astype(jnp.float32)
    diff_w = diff_weight.astype(jnp.float32)
    deep = tuple(
        (
            item.astype(jnp.float32)
            for item in (
                w_reduce,
                gain_one,
                bias_one,
                w_spatial,
                gain_two,
                bias_two,
                w_expand,
                gain_three,
                bias_three,
                w_squeeze,
                w_fine,
                w_coarse,
                w_excite,
            )
        )
    )
    pre, pull_front = jax.vjp(
        lambda first_w, second_w: stem_front(frames32, first_w, second_w), stem_w, diff_w
    )
    stem_count = float(pre.shape[0] * pre.shape[1] * pre.shape[2] * parts)
    stem_sums, stem_back_sums = synced(pre, 1.0)
    stem_result, pull_rear = jax.vjp(
        partial(stem_rear, count=stem_count, layout=stem_cotangent.shape),
        pre,
        stem_sums,
        stem_gain,
        stem_bias,
    )
    inputs = features.astype(jnp.float32) * mask
    block_result, unused = deep_forward(inputs, mask, count, deep)
    again_result, pulls = deep_forward(inputs, mask, count, deep)
    g_inputs, deep_grads = deep_backward(block_cotangent.astype(jnp.float32), pulls)
    grad_feats = (g_inputs * mask).astype(jnp.bfloat16)
    g_pre, g_sums, g_gain, g_bias = pull_rear(stem_cotangent.astype(jnp.float32))
    g_pre = grad_round(g_pre + synced_back(g_sums, stem_back_sums))
    g_stem_w, g_diff_w = pull_front(g_pre)
    every_grad = [g_stem_w, g_diff_w, g_gain, g_bias] + deep_grads
    shares = lax.psum_scatter(
        pack_grads(every_grad, parts), ("clip", "seg"), scatter_dimension=0, tiled=True
    )
    totals = unpack_grads(
        lax.all_gather(shares.astype(jnp.bfloat16), ("clip", "seg"), axis=0, tiled=True).astype(
            shares.dtype
        ),
        every_grad,
    )
    return tuple(
        [stem_result.astype(jnp.bfloat16), block_result.astype(jnp.bfloat16), grad_feats] + totals
    )


def solution(mesh):
    placed = (
        P("clip", "seg", None, None, None, None),
        P("clip", "seg", None, None, None),
        P(),
        P(),
        P(),
        P(),
        P(),
        P(),
        P(),
        P(),
        P(),
        P(),
        P(),
        P(),
        P(),
        P(),
        P(),
        P(),
        P(),
        P(),
        P("clip", "seg", None, None, None),
        P("clip", "seg", None, None, None),
    )
    return jax.shard_map(
        shards,
        mesh=mesh,
        in_specs=placed,
        out_specs=(
            P("clip", "seg", None, None, None),
            P("clip", "seg", None, None, None),
            P("clip", "seg", None, None, None),
            P(),
            P(),
            P(),
            P(),
            P(),
            P(),
            P(),
            P(),
            P(),
            P(),
            P(),
            P(),
            P(),
            P(),
            P(),
            P(),
            P(),
        ),
        check_vma=False,
    )
```

profile of v0, /device:TPU:0, one launch (start us, length us, event | category | flops | bytes accessed | tf_op | source)
XLA Modules:
  0.0 1023.0 jit_solution(309566943067462256)
XLA Ops:
  10.2 2.7 multiply_reduce_fusion.7
  12.9 42.0 %all-reduce.11 = (f32[512]{0:T(512)S(1)}, f32[512]{0:T(512)S(1)}) all-reduce(f32[512]{0:T(512)S(1)} %get-tuple-element.139, f32[512]{0:T(512)S(1)} %get-tuple-element.138), channel_id=1, replica_groups=mesh['clip'=8,'seg'=4] {'clip','seg'}, use_global_device_ids=true, to_apply=%region_9.10 | all-reduce | flops 1024 | bytes 8192 | tf_op jit(solution)/shard_map/psum | solution.py:104
  56.4 4.5 fusion.87
  61.2 40.2 %all-reduce.10 = (f32[512]{0:T(512)S(1)}, f32[512]{0:T(512)S(1)}) all-reduce(f32[512]{0:T(512)S(1)} %get-tuple-element.137, f32[512]{0:T(512)S(1)} %get-tuple-element.136), channel_id=1, replica_groups=mesh['clip'=8,'seg'=4] {'clip','seg'}, use_global_device_ids=true, to_apply=%region_13.14 | all-reduce | flops 1024 | bytes 8192 | tf_op jit(solution)/shard_map/psum | solution.py:104
  102.3 2.3 multiply_reduce_fusion
  104.6 40.2 %all-reduce.9 = (f32[2048]{0:T(1024)S(1)}, f32[2048]{0:T(1024)S(1)}) all-reduce(f32[2048]{0:T(1024)S(1)} %get-tuple-element.126, f32[2048]{0:T(1024)S(1)} %get-tuple-element.125), channel_id=1, replica_groups=mesh['clip'=8,'seg'=4] {'clip','seg'}, use_global_device_ids=true, to_apply=%region_17.18 | all-reduce | flops 4096 | bytes 32768 | tf_op jit(solution)/shard_map/psum | solution.py:104
  144.9 2.2 convert_bitcast_fusion
  150.0 3.8 collective-permute-start
  154.8 4.6 copy.238
  159.4 5.1 pad.17
  164.5 6.9 copy.189
  174.1 2.1 copy.190
  176.1 2.7 convolution_select_fusion
  178.9 2.1 copy.192
  180.9 10.9 %reshape.547 = f32[4,12,4,12,4,12]{4,3,2,1,5,0:T(8,128)} reshape(f32[4,1,48,48,4,3]{3,2,5,4,1,0:T(8,128)S(1)} %fusion.49) | data formatting | bytes 884736 | tf_op jit(solution)/shard_map/jvp()/reshape;jvp()/reshape | solution.py:60
  191.9 8.1 reduce_sum.280
  217.8 2.4 fusion.22
  220.7 2.4 fusion.36
  231.8 3.3 collective-permute-start.2
  243.1 4.4 fusion.23
  248.1 41.4 %all-reduce.8 = (f32[2048]{0:T(1024)}, f32[2048]{0:T(1024)}) all-reduce(f32[2048]{0:T(1024)} %get-tuple-element.197, f32[2048]{0:T(1024)} %get-tuple-element.196), channel_id=1, replica_groups=mesh['clip'=8,'seg'=4] {'clip','seg'}, use_global_device_ids=true, to_apply=%region_25.26 | all-reduce | flops 4096 | bytes 32768 | tf_op jit(solution)/shard_map/psum | solution.py:108
  289.6 5.6 fusion.58
  295.3 2.5 multiply_reduce_fusion.8
  297.8 3.0 convolution_bitcast_fusion.3
  300.9 40.9 %all-reduce.7 = (f32[64]{0:T(128)S(1)}, f32[64]{0:T(128)S(1)}, f32[512]{0:T(512)S(1)}, f32[512]{0:T(512)S(1)}) all-reduce(f32[64]{0:T(128)S(1)} %copy-done.95, f32[64]{0:T(128)S(1)} %copy-done.94, f32[512]{0:T(512)S(1)} %get-tuple-element.203, f32[512]{0:T(512)S(1)} %get-tuple-element.202), channel_id=1, replica_groups=mesh['clip'=8,'seg'=4] {'clip','seg'}, use_global_device_ids=true, to_apply=%region_4.5 | all-reduce | flops 1152 | bytes 9216 | tf_op jit(solution)/shard_map/psum | solution.py:104
  342.1 4.5 fusion.97
  346.6 6.1 fusion.85
  352.8 2.9 copy.241
  359.1 40.3 %all-reduce.6 = (f32[64]{0:T(128)S(1)}, f32[64]{0:T(128)S(1)}, f32[512]{0:T(512)S(1)}, f32[512]{0:T(512)S(1)}) all-reduce(f32[64]{0:T(128)S(1)} %fusion.132, f32[64]{0:T(128)S(1)} %get-tuple-element.161, f32[512]{0:T(512)S(1)} %get-tuple-element.201, f32[512]{0:T(512)S(1)} %get-tuple-element.200), channel_id=1, replica_groups=mesh['clip'=8,'seg'=4] {'clip','seg'}, use_global_device_ids=true, to_apply=%region_37.38 | all-reduce | flops 1152 | bytes 9216 | tf_op jit(solution)/shard_map/psum | solution.py:108
  400.5 4.2 fusion.10
  409.1 3.1 copy.239
  412.2 9.9 copy.240
  422.1 183.1 %concatenate.10 = f32[5298240]{0:T(1024)} concatenate(f32[9408]{0:T(1024)S(1)} %reshape.572, f32[6912]{0:T(1024)S(1)} %reshape.576, f32[64]{0:T(128)S(1)} %get-tuple-element.122, f32[64]{0:T(128)S(1)} %get-tuple-element.129, f32[1048576]{0:T(1024)} %bitcast.288, f32[512]{0:T(512)S(1)} %get-tuple-element.134, f32[512]{0:T(512)S(1)} %get-tuple-element.143, f32[2359296]{0:T(1024)} %bitcast.286, ...), dimensions={0} | concatenate | bytes 42385920 | tf_op jit(solution)/shard_map/concatenate | solution.py:232
  605.2 15.5 %pad_bitcast_fusion = f32[41408,128]{1,0:T(8,128)} fusion(f32[5298240]{0:T(1024)} %concatenate.10), kind=kLoop, calls=%fused_computation.1 | loop fusion | bytes 42393856 | tf_op jit(solution)/shard_map/reshape | solution.py:235
  620.8 228.2 %fusion = f32[1296,128]{1,0:T(8,128)} fusion(f32[41408,128]{1,0:T(8,128)} %pad_bitcast_fusion), kind=kCustom, calls=%all-reduce-scatter | all-reduce-scatter fusion | flops 5308417 | bytes 21864448
  849.9 6.4 collective-permute-start.4
  856.4 3.0 concatenate.12
  860.3 2.0 copy.226
  862.3 5.5 fusion.9
  867.9 82.1 %all-gather.3.cloned.1.call-done = bf16[32,1294,128]{2,1,0:T(8,128)(2,1)} async-done(((bf16[1,1294,128]{2,1,0:T(8,128)(2,1)}), bf16[32,1294,128]{2,1,0:T(8,128)(2,1)}) %all-gather.3.cloned.1.call-update) | async-done | bytes 10600464 | tf_op jit(solution)/shard_map/all_gather | solution.py:325
  950.0 12.7 %reshape.608 = f32[5300224]{0:T(1024)} reshape(bf16[32,1294,128]{2,1,0:T(8,128)(2,1)} %all-gather.3.cloned.1.call-done) | data formatting | bytes 31801344 | tf_op jit(solution)/shard_map/reshape | solution.py:239
  967.6 2.6 fusion.151
  970.3 3.1 fusion.150
  973.4 9.0 fusion.153
  982.4 9.5 slice.130
  994.5 11.2 %reshape.590 = f32[3,3,512,512]{3,2,1,0:T(8,128)} reshape(f32[2359296]{0:T(1024)} %slice.130) | data formatting | bytes 18874368 | tf_op jit(solution)/shard_map/reshape | solution.py:243
  1005.7 4.9 reshape.591
  1010.6 5.1 reshape.589
  (303 shorter events, 65.0 us)
Async XLA Ops:
  7.2 95.0 %copy-start = (bf16[512,2048]{1,0:T(8,128)(2,1)S(1)}, bf16[512,2048]{1,0:T(8,128)(2,1)}, u32[]{:S(2)}) copy-start(bf16[512,2048]{1,0:T(8,128)(2,1)} %param.35) | copy-start | bytes 6291460
  7.2 942.8 %all-gather.3.cloned.1.call-start = ((), (), s32[]{:S(2)}) async-start(), calls=%async_computation | async-start | bytes 10948608 | tf_op jit(solution)/shard_map/all_gather | solution.py:325
  10.2 45.3 %copy-start.63 = (f32[512]{0:T(512)S(1)}, f32[512]{0:T(512)}, u32[]{:S(2)}) copy-start(f32[512]{0:T(512)} %param.30) | copy-start | bytes 6148
  10.2 45.3 %copy-start.71 = (f32[512]{0:T(512)S(1)}, f32[512]{0:T(512)}, u32[]{:S(2)}) copy-start(f32[512]{0:T(512)} %param.31) | copy-start | bytes 6148
  12.9 48.0 %copy-start.8 = (f32[4,8,8,512]{3,2,1,0:T(8,128)}, f32[4,8,8,512]{3,2,1,0:T(8,128)S(1)}, u32[]{:S(2)}) copy-start(f32[4,8,8,512]{3,2,1,0:T(8,128)S(1)} %get-tuple-element.207) | copy-start | bytes 1572868
  56.4 45.5 %copy-start.76 = (f32[512]{0:T(512)S(1)}, f32[512]{0:T(512)}, u32[]{:S(2)}) copy-start(f32[512]{0:T(512)} %param.33) | copy-start | bytes 6148
  56.4 45.5 %copy-start.89 = (f32[512]{0:T(512)S(1)}, f32[512]{0:T(512)}, u32[]{:S(2)}) copy-start(f32[512]{0:T(512)} %param.34) | copy-start | bytes 6148
  61.0 43.6 %copy-start.10 = (f32[4,8,8,512]{3,0,2,1:T(4,128)}, f32[4,8,8,512]{3,0,2,1:T(4,128)S(1)}, u32[]{:S(2)}) copy-start(f32[4,8,8,512]{3,0,2,1:T(4,128)S(1)} %fusion.87) | copy-start | bytes 1572868
  102.2 42.6 %copy-start.49 = (f32[2048]{0:T(1024)S(1)}, f32[2048]{0:T(1024)}, u32[]{:S(2)}) copy-start(f32[2048]{0:T(1024)} %param.36) | copy-start | bytes 24580
  102.3 42.6 %copy-start.57 = (f32[2048]{0:T(1024)S(1)}, f32[2048]{0:T(1024)}, u32[]{:S(2)}) copy-start(f32[2048]{0:T(1024)} %param.37) | copy-start | bytes 24580
  104.6 42.5 %copy-start.97 = (bf16[2048,128]{1,0:T(8,128)(2,1)S(1)}, bf16[2048,128]{1,0:T(8,128)(2,1)}, u32[]{:S(2)}) copy-start(bf16[2048,128]{1,0:T(8,128)(2,1)} %param.38) | copy-start | bytes 1572868
  147.1 6.8 copy-start.23
  148.7 54.3 %collective-permute-start.1 = (bf16[4,1,8,8,128]{4,3,2,0,1:T(8,128)(2,1)}, bf16[4,1,8,8,128]{4,3,2,0,1:T(8,128)(2,1)}, u32[]{:S(2)}, u32[]{:S(2)}) collective-permute-start(bf16[4,1,8,8,128]{4,3,2,0,1:T(8,128)(2,1)} %fusion.99), channel_id=1, source_target_pairs={{1,0},{2,1},{3,2},{5,4},{6,5},{7,6},{9,8},{10,9},{11,10},{13,12},{... | collective-permute-start | bytes 196616 | tf_op jit(solution)/shard_map/ppermute | solution.py:19
  150.0 53.0 %collective-permute-start = (bf16[4,1,8,8,128]{4,3,2,0,1:T(8,128)(2,1)}, bf16[4,1,8,8,128]{4,3,2,0,1:T(8,128)(2,1)}, u32[]{:S(2)}, u32[]{:S(2)}) collective-permute-start(bf16[4,1,8,8,128]{4,3,2,0,1:T(8,128)(2,1)} %fusion.99), channel_id=1, source_target_pairs={{0,1},{1,2},{2,3},{4,5},{5,6},{6,7},{8,9},{9,10},{10,11},{12,13},{... | collective-permute-start | bytes 196616 | tf_op jit(solution)/shard_map/ppermute | solution.py:17
  191.9 8.6 copy-start.99
  209.4 4.8 copy-start.19
  209.4 6.2 copy-start.35
  227.7 8.8 copy-start.29
  227.7 8.8 copy-start.32
  227.7 8.9 copy-start.100
  231.8 8.5 collective-permute-start.2
  235.1 5.2 collective-permute-start.3
  243.1 4.4 copy-start.68
  243.1 4.4 copy-start.70
  289.6 5.7 copy-start.11
  289.6 5.7 copy-start.74
  289.6 5.7 copy-start.77
  289.6 5.7 copy-start.80
  289.6 5.7 copy-start.90
  297.8 44.0 %copy-start.12 = (f32[4,8,8,512]{3,0,2,1:T(4,128)S(1)}, f32[4,8,8,512]{3,0,2,1:T(4,128)}, u32[]{:S(2)}) copy-start(f32[4,8,8,512]{3,0,2,1:T(4,128)} %copy-done.10) | copy-start | bytes 1572868
  297.8 44.0 %copy-start.36 = (f32[4,8,8,512]{3,2,1,0:T(8,128)S(1)}, f32[4,8,8,512]{3,2,1,0:T(8,128)}, u32[]{:S(2)}) copy-start(f32[4,8,8,512]{3,2,1,0:T(8,128)} %get-tuple-element.210) | copy-start | bytes 1572868
  297.8 44.0 %copy-start.75 = (f32[512]{0:T(512)S(1)}, f32[512]{0:T(512)}, u32[]{:S(2)}) copy-start(f32[512]{0:T(512)} %copy-done.73) | copy-start | bytes 6148
  297.8 44.0 %copy-start.78 = (f32[512]{0:T(512)S(1)}, f32[512]{0:T(512)}, u32[]{:S(2)}) copy-start(f32[512]{0:T(512)} %param.33) | copy-start | bytes 6148
  346.6 6.1 copy-start.18
  412.1 9.9 copy-start.17
  412.1 9.9 copy-start.21
  412.1 9.9 copy-start.87
  412.2 9.9 copy-start.88
  412.2 9.9 copy-start.91
  412.2 9.9 copy-start.92
  849.0 13.3 %copy-start.5 = (f32[4,8,8,2048]{3,2,1,0:T(8,128)S(1)}, f32[4,8,8,2048]{3,2,1,0:T(8,128)}, u32[]{:S(2)}) copy-start(f32[4,8,8,2048]{3,2,1,0:T(8,128)} %get-tuple-element.208) | copy-start | bytes 6291460
  849.0 13.3 %copy-start.44 = (f32[2048]{0:T(1024)S(1)}, f32[2048]{0:T(1024)}, u32[]{:S(2)}) copy-start(f32[2048]{0:T(1024)} %copy-done.41) | copy-start | bytes 24580
  849.0 13.3 %copy-start.52 = (f32[2048]{0:T(1024)S(1)}, f32[2048]{0:T(1024)}, u32[]{:S(2)}) copy-start(f32[2048]{0:T(1024)} %param.36) | copy-start | bytes 24580
  849.0 13.3 %copy-start.56 = (f32[2048]{0:T(1024)S(1)}, f32[2048]{0:T(1024)}, u32[]{:S(2)}) copy-start(f32[2048]{0:T(1024)} %copy-done.53) | copy-start | bytes 24580
  849.0 13.3 %copy-start.60 = (f32[2048]{0:T(1024)S(1)}, f32[2048]{0:T(1024)}, u32[]{:S(2)}) copy-start(f32[2048]{0:T(1024)} %param.37) | copy-start | bytes 24580
  849.9 6.5 collective-permute-start.4
  982.4 10.3 %slice-start = ((f32[5300224]{0:T(1024)}), f32[9408]{0:T(1024)S(1)}, s32[]{:S(2)}) async-start(f32[5300224]{0:T(1024)} %reshape.608), calls=%async_computation.1 | async-start | bytes 81920 | tf_op jit(solution)/shard_map/slice | solution.py:243
  1010.6 5.1 copy-start.1
  (60 other events, 143.0 us)
Sparse Core Ops, SparseCore 0:
  860.5 89.4 all-gather.2
where the time goes:
time: 1040 us; the launch traced here: 1020 us
  blocking collectives  473 us (45%)
  local copies, waits for them, and re-layouts  327 us (31%)
  waiting for transfers between devices  82.2 us (8%)
  matrix products  64.2 us (6%)
  other arithmetic  43.7 us (4%)
  between operations  16.5 us (2%)
  starting transfers between devices  16.2 us (2%)
    unnamed x1, blocking collectives  228 us
    concatenate x1, local copies, waits for them, and re-layouts, pack_grads(): flat = jnp.concatenate([grad.reshape(-1) for grad in grads])  183 us
    psum x4, blocking collectives, synced(): return (lax.psum(local_sums, ('clip', 'seg')), pull_sums)  163 us
    all_gather x1, waiting for transfers between devices, shards(): lax.all_gather(shares.astype(jnp.bfloat16), ('clip', 'seg'), axis=0, tile...  82.1 us
    psum x2, blocking collectives, synced_back(): return pull_sums(lax.psum(grad_sums, ('clip', 'seg')))[0]  81.8 us
    conv_general_dilated x17, matrix products, convolve(): lax.conv_general_dilated(image, kernel, (stride, stride), 'SAME', dimensi...  36.7 us
    unnamed x212, local copies, waits for them, and re-layouts  33.3 us
    slice x10, local copies, waits for them, and re-layouts, unpack_grads(): pieces.append(flat[offset:offset + grad.size].reshape(grad.shape))  29.3 us
  transfers between devices with their start and end apart: 6, of which 2 were waited for; matrix products, arithmetic and copies ran while one was open for 6% of the time, Pallas kernels for 0%

commit v1 on v0

v1 whole, which is shorter than its diff:
```python
from functools import partial
from types import SimpleNamespace

import jax
import jax.numpy as jnp
from jax import lax
from jax.experimental import pallas as pl
from jax.experimental.pallas import tpu as pltpu
from jax.sharding import PartitionSpec as P

MESH = pl.DeviceIdType.MESH
F32, BF16 = jnp.float32, jnp.bfloat16
LANES = 128
BLOCK = 64
PAD = 16
TAPS = [(di, dj) for di in (-1, 0, 1) for dj in (-1, 0, 1)]


def dot(a, b):
    return lax.dot_general(a, b, (((1,), (0,)), ((), ())), preferred_element_type=F32)


def dot_bt(a, b):
    return lax.dot_general(a, b, (((1,), (1,)), ((), ())), preferred_element_type=F32)


def dot_at(a, b):
    return lax.dot_general(a, b, (((0,), (0,)), ((), ())), preferred_element_type=F32)


def columns(total, body, step=LANES):
    def go(j, carry):
        body(pl.multiple_of(j * step, step), j)
        return carry

    lax.fori_loop(0, total // step, go, 0)


def lanes(start, size=LANES):
    return pl.ds(start, size)


def fold(block):
    return block.reshape(block.shape[0] // 8, 8, LANES).sum(axis=0)


def total_of(part):
    return jnp.sum(part, axis=0, keepdims=True)


class Sems:
    def __init__(self, ref):
        self.ref, self.used = ref, 0

    def take(self):
        self.used += 1
        return self.ref.at[self.used - 1]


class Place:
    def __init__(self, clips, segs):
        self.clips, self.segs = clips, segs
        self.clip, self.seg = lax.axis_index("clip"), lax.axis_index("seg")
        self.near = 2 * segs
        self.far = clips // 2
        self.near_me = lax.rem(self.clip, 2) * segs + self.seg
        self.far_me = self.clip // 2

    def near_device(self, t):
        return ((self.clip // 2) * 2 + t // self.segs, lax.rem(t, self.segs))

    def far_device(self, t):
        return (t * 2 + lax.rem(self.clip, 2), self.seg)

    def bit(self, axis, stride):
        mine = self.seg if axis == "seg" else self.clip
        bit = lax.rem(mine // stride, 2)
        other = mine + stride * (1 - 2 * bit)
        return bit, (self.clip, other) if axis == "seg" else (other, self.seg)

    def greet(self):
        sem = pltpu.get_barrier_semaphore()

        def near(k, carry):
            pl.semaphore_signal(
                sem, inc=1, device_id=self.near_device(lax.rem(self.near_me + k, self.near)), device_id_type=MESH
            )
            return carry

        def far(k, carry):
            pl.semaphore_signal(
                sem, inc=1, device_id=self.far_device(lax.rem(self.far_me + k, self.far)), device_id_type=MESH
            )
            return carry

        lax.fori_loop(1, self.near, near, 0)
        lax.fori_loop(1, self.far, far, 0)
        pl.semaphore_wait(sem, self.near + self.far - 2)


def remote(src, dst, sends, recvs, device):
    copy = pltpu.make_async_remote_copy(
        src_ref=src,
        dst_ref=dst,
        send_sem=sends.take(),
        recv_sem=recvs.take(),
        device_id=device,
        device_id_type=MESH,
    )
    copy.start()
    return copy


class Sums:
    def __init__(self, place, near_buf, far_buf, result, sends, recvs):
        self.place, self.near_buf, self.far_buf, self.result = place, near_buf, far_buf, result
        self.sends, self.recvs = sends, recvs

    def put(self, row, at, value):
        self.near_buf[self.place.near_me, row : row + 1, lanes(at, value.shape[1])] = value

    def _send(self, buf, me, count, device):
        mine = buf.at[me]
        return [remote(mine, mine, self.sends, self.recvs, device(lax.rem(me + k, count))) for k in range(1, count)]

    def _add(self, buf, count):
        value = buf[0]
        for k in range(1, count):
            value = value + buf[k]
        return value

    def start(self):
        p = self.place
        self.copies = self._send(self.near_buf, p.near_me, p.near, p.near_device)

    def middle(self):
        p = self.place
        for copy in self.copies:
            copy.wait()
        self.far_buf[p.far_me] = self._add(self.near_buf, p.near)
        self.copies = self._send(self.far_buf, p.far_me, p.far, p.far_device)

    def finish(self):
        for copy in self.copies:
            copy.wait()
        self.result[...] = self._add(self.far_buf, self.place.far)


def bit_order(clips, segs, kind):
    seg = [("seg", 1 << k) for k in range(segs.bit_length() - 1)]
    clip = [("clip", 1 << k) for k in range(clips.bit_length() - 1)]
    if kind == 0:
        return seg[:1] + clip[:1] + seg[1:] + clip[1:]
    return seg + clip


def halvings(rows, order):
    steps = []
    for _ in order:
        half = rows // 2
        if rows % 2 == 0 and half % 16 == 0:
            steps.append((rows, half, True))
            rows = half
        else:
            steps.append((rows, rows, False))
    return steps


class Job:
    def __init__(self, place, grads, landing, packed, base, rows, order, land, local, sends, recvs):
        self.grads, self.landing, self.packed = grads, landing, packed
        self.local, self.sends, self.recvs = local, sends, recvs
        self.steps = []
        at = base
        for (axis, stride), (size, sent, halved) in zip(order, halvings(rows, order)):
            bit, device = place.bit(axis, stride)
            if halved:
                keep, away = at + bit * sent, at + (1 - bit) * sent
            else:
                keep, away = at, at
            self.steps.append((keep, away, sent, halved, device, land))
            land += sent
            at = keep
        self.land_end = land
        self.at = 0

    def _rows(self, ref, start, size):
        return ref.at[pl.ds(pl.multiple_of(start, 16), size)]

    def scatter_start(self):
        keep, away, size, halved, device, land = self.steps[self.at]
        self.copy = remote(
            self._rows(self.grads, away, size), self._rows(self.landing, land, size), self.sends, self.recvs, device
        )

    def scatter_finish(self):
        keep, away, size, halved, device, land = self.steps[self.at]
        self.copy.wait()
        block = 32 if size % 32 == 0 else 16

        def add(k, carry):
            mine = pl.ds(pl.multiple_of(keep + k * block, 16), block)
            theirs = pl.ds(pl.multiple_of(land + k * block, 16), block)
            self.grads[mine] = (self.grads[mine].astype(F32) + self.landing[theirs].astype(F32)).astype(BF16)
            return carry

        lax.fori_loop(0, size // block, add, 0)
        self.at += 1

    def own_start(self):
        keep, away, size, halved, device, land = self.steps[-1]
        self.copy = pltpu.make_async_copy(
            self._rows(self.grads, keep, size), self._rows(self.packed, keep, size), self.local.take()
        )
        self.copy.start()

    def own_finish(self):
        self.copy.wait()

    def gather_start(self):
        keep, away, size, halved, device, land = self.steps[self.at - 1]
        self.copy = None
        if halved:
            mine = self._rows(self.packed, keep, size)
            self.copy = remote(mine, mine, self.sends, self.recvs, device)

    def gather_finish(self):
        self.at -= 1
        if self.copy is not None:
            self.copy.wait()


def landing_rows(rows, order):
    return sum(sent for _, sent, _ in halvings(rows, order))


class Stem:
    KERNEL = 7
    COLOURS = 3

    def __init__(self, R, S, images, side, count):
        self.R, self.S, self.images, self.side, self.count = R, S, images, side, count
        self.cells = side // 2
        self.pairs = self.cells // 2
        self.band = side * 8
        self.fine = self.COLOURS * self.band
        self.half_rows = images * self.pairs
        self.depth = S.xx.shape[1]
        self.spread = (self.depth - self.fine) // 3

    def _table(self, q):
        per = self.S.grads.shape[1] // LANES
        return q // per * self.depth, lanes(q % per * LANES)

    def tables(self):
        R, S = self.R, self.S
        table, wt, wd = S.grads, S.wt, S.wd
        tall = 32
        used = self.depth * self.pairs * LANES // table.shape[1]

        def clear(k, carry):
            table[pl.ds(pl.multiple_of(k * tall, tall), tall)] = jnp.zeros((tall, table.shape[1]), BF16)
            return carry

        lax.fori_loop(0, used // tall, clear, 0)
        wt[...] = jnp.zeros(wt.shape, F32)
        wd[...] = jnp.zeros(wd.shape, F32)
        weights = R.stem_w[...].astype(F32)
        for ki in range(self.KERNEL):
            for c in range(self.COLOURS):
                for kj in range(self.KERNEL):
                    at = c * 64 + kj * 8 + ki
                    wt[at : at + 1, 0:64] = weights[ki * self.COLOURS + c, kj : kj + 1]
        for c in range(self.COLOURS):
            for p in range(5):
                block = jnp.zeros((16, LANES), F32)
                if p < 4:
                    block = block + wt[c * 64 + 16 * p : c * 64 + 16 * p + 16, :]
                if p > 0:
                    high = wt[c * 64 + 16 * p - 16 : c * 64 + 16 * p, :]
                    block = block + pltpu.roll(high, 64, 1)
                block = block.astype(BF16)
                for q in range(self.pairs):
                    j = 4 * q - 2 + 2 * p
                    if 0 <= j < self.side:
                        top, at = self._table(q)
                        top = top + c * self.band + j * 8
                        table[top : top + 16, at] = block
        weights = R.diff_w[...].astype(F32)
        for t in range(9):
            wd[t * 16 : t * 16 + weights.shape[1], 0:64] = weights[t]
        for ki in range(3):
            for kj in range(3):
                block = wd[(ki * 3 + kj) * 16 : (ki * 3 + kj) * 16 + 16, :]
                block = (block + pltpu.roll(block, 64, 1)).astype(BF16)
                for q in range(self.pairs):
                    j = q + kj - 1
                    if 0 <= j < self.pairs:
                        top, at = self._table(q)
                        top = top + self.fine + ki * self.spread + j * 16
                        table[top : top + 16, at] = block

    def patches(self):
        S, side, images = self.S, self.side, self.images
        frames, padded, taps, xx = S.frames, S.padded, S.stem_taps, S.xx
        tall = padded.shape[0] // images
        padded[...] = jnp.zeros(padded.shape, F32)
        taps[...] = jnp.zeros(taps.shape, F32)
        row = lax.broadcasted_iota(jnp.int32, (taps.shape[1], self.band), 0)
        lane = lax.broadcasted_iota(jnp.int32, (taps.shape[1], self.band), 1)
        place = jnp.where(row == lax.rem(lane, 8) * 64 + lane // 8, 1.0, 0.0).astype(BF16)
        for c in range(self.COLOURS):
            for img in range(images):
                plane = frames[(img * 5 + 2) * self.COLOURS + c].astype(F32)
                padded[img * tall + 2 : img * tall + 2 + side, 0:side] = plane
            for ki in range(self.KERNEL):
                for parity in range(2):
                    for img in range(images):
                        start = img * tall + 2 * parity + ki
                        piece = padded[pl.ds(start, self.pairs, stride=4), 0:64]
                        top = parity * self.half_rows + img * self.pairs
                        taps[top : top + self.pairs, ki * 64 : ki * 64 + 64] = piece
            xx[:, lanes(c * self.band, self.band)] = dot(taps[...].astype(BF16), place).astype(BF16)
        row = lax.broadcasted_iota(jnp.int32, (side, self.spread), 0)
        lane = lax.broadcasted_iota(jnp.int32, (side, self.spread), 1)
        inside = row // 4 == lane // 16
        channel = lax.rem(lane, 16)
        total = None
        for f in range(5):
            for c in range(self.COLOURS):
                sign = jnp.zeros((side, self.spread), F32)
                if f > 0:
                    sign = sign + jnp.where(channel == (f - 1) * self.COLOURS + c, 1.0, 0.0)
                if f < 4:
                    sign = sign - jnp.where(channel == f * self.COLOURS + c, 1.0, 0.0)
                sign = jnp.where(inside, sign, 0.0).astype(BF16)
                planes = jnp.concatenate(
                    [frames[(img * 5 + f) * self.COLOURS + c] for img in range(images)], axis=0
                )
                part = dot(planes, sign)
                total = part if total is None else total + part
        for h in range(self.spread // LANES):
            S.columns[h] = total[:, h * LANES : (h + 1) * LANES]
        pooled = None
        for k in range(4):
            parts = [
                S.columns[h, pl.ds(k, self.half_rows, stride=4), :] for h in range(self.spread // LANES)
            ]
            part = jnp.concatenate(parts, axis=1)
            pooled = part if pooled is None else pooled + part
        pooled = (pooled * 0.0625).astype(BF16).astype(F32)
        row = lax.rem(lax.broadcasted_iota(jnp.int32, pooled.shape, 0), self.pairs)
        for ki in range(3):
            rolled = pltpu.roll(pooled, (1 - ki) % self.half_rows, 0)
            ok = (row + ki - 1 >= 0) & (row + ki - 1 < self.pairs)
            rolled = jnp.where(ok, rolled, 0.0).astype(BF16)
            at = lanes(self.fine + ki * self.spread, self.spread)
            xx[0 : self.half_rows, at] = rolled
            xx[self.half_rows :, at] = rolled

    def forward(self, sums, at):
        S, per = self.S, self.S.grads.shape[1]
        for n in range(self.pairs * LANES // per):
            S.pre[:, lanes(n * per, per)] = dot(S.xx[...], S.grads[n * self.depth : (n + 1) * self.depth, :])
        s = q = jnp.zeros((8, LANES), F32)
        for k in range(self.pairs):
            v = S.pre[:, lanes(k * LANES)]
            s, q = s + fold(v), q + fold(v * v)
        self._put(sums, at, s, q)

    def _put(self, sums, at, s, q):
        for row, part in enumerate((s, q)):
            part = total_of(part)
            sums.put(row, at, part + pltpu.roll(part, 64, 1))

    def _norm(self):
        S, inv = self.S, 1.0 / self.count
        mean = S.stem_stat[0:1, :] * inv
        root = lax.rsqrt(S.stem_stat[1:2, :] * inv - mean * mean + 1e-05)
        gain, bias = self.R.stem_gain[...], self.R.stem_bias[...]
        scale = root * jnp.concatenate([gain, gain], axis=1)
        return scale, jnp.concatenate([bias, bias], axis=1) - mean * scale, mean, root

    def rear(self, stat, sums, at):
        S = self.S
        S.stem_stat[...] = stat
        scale, shift, mean, root = self._norm()
        step = 2 * self.cells
        S.stem_wide[:, 0:64] = S.stem_cot[...].astype(F32)
        s = q = jnp.zeros((8, LANES), F32)
        for k in range(self.pairs):
            pre = S.pre[:, lanes(k * LANES)]
            cot = []
            for parity in range(2):
                pieces = [
                    S.stem_wide[pl.ds(parity * self.cells + 2 * k + i, self.half_rows, stride=step), 0:64]
                    for i in range(2)
                ]
                cot.append(jnp.concatenate(pieces, axis=1))
            y = pre * scale + shift
            sg = jax.nn.sigmoid(y)
            out = y * sg
            g = jnp.concatenate(cot, axis=0) * (sg + out * (1.0 - sg))
            S.gpre[:, lanes(k * LANES)] = g
            s, q = s + fold(g), q + fold(g * ((pre - mean) * root))
            swapped = pltpu.roll(out, 64, 1)
            for parity in range(2):
                rows = slice(parity * self.half_rows, (parity + 1) * self.half_rows)
                for i, half in enumerate((out, swapped)):
                    where = pl.ds(parity * self.cells + 2 * k + i, self.half_rows, stride=step)
                    S.stem_wide[where, :] = half[rows]
        S.stem_cot[...] = S.stem_wide[:, 0:64].astype(BF16)
        self._put(sums, at, s, q)

    def back(self, stat, top):
        S, inv = self.S, 1.0 / self.count
        scale, _, mean, root = self._norm()
        gb, gg = stat[0:1, :] * inv, stat[1:2, :] * inv
        bands, spots = S.bands, S.spots
        bands[...] = jnp.zeros(bands.shape, F32)
        spots[...] = jnp.zeros(spots.shape, F32)
        for k in range(self.pairs):
            hat = (S.pre[:, lanes(k * LANES)] - mean) * root
            g = (scale * (S.gpre[:, lanes(k * LANES)] - gb - hat * gg)).astype(BF16)
            S.prod[...] = dot_at(S.xx[...], g)
            for c in range(self.COLOURS):
                for p in range(5):
                    j = 4 * k - 2 + 2 * p
                    if 0 <= j < self.side:
                        here = slice((c * 5 + p) * 16, (c * 5 + p) * 16 + 16)
                        start = c * self.band + j * 8
                        bands[here] = bands[here] + S.prod[start : start + 16]
            for ki in range(3):
                for kj in range(3):
                    j = k + kj - 1
                    if 0 <= j < self.pairs:
                        here = slice((ki * 3 + kj) * 16, (ki * 3 + kj) * 16 + 16)
                        start = self.fine + ki * self.spread + j * 16
                        spots[here] = spots[here] + S.prod[start : start + 16]
        low = lax.broadcasted_iota(jnp.int32, (8, LANES), 1) < 64
        for c in range(self.COLOURS):
            for kj in range(self.KERNEL):
                first = bands[c * 80 + kj * 8 : c * 80 + kj * 8 + 8]
                other = bands[c * 80 + kj * 8 + 16 : c * 80 + kj * 8 + 24]
                at = (c * self.KERNEL + kj) * 8
                S.wt[at : at + 8] = jnp.where(low, first + pltpu.roll(other, 64, 1), 0.0)
        grads = S.grads
        grads[top : top + LANES, :] = jnp.zeros((LANES, grads.shape[1]), BF16)
        rest = S.wt.shape[0] - LANES
        used = self.COLOURS * self.KERNEL * 8
        S.wt[used:] = jnp.zeros((S.wt.shape[0] - used, LANES), F32)
        grads[top : top + LANES, lanes(0)] = S.wt[0:LANES].astype(BF16)
        grads[top : top + rest, lanes(LANES)] = S.wt[LANES:].astype(BF16)
        both = spots[...] + pltpu.roll(spots[...], 64, 1)
        grads[top : top + LANES, lanes(2 * LANES)] = both[0:LANES].astype(BF16)
        grads[top : top + 16, lanes(3 * LANES)] = both[LANES:].astype(BF16)


class Layout:
    def __init__(self, wide, mid, red):
        self.excite = 0
        self.scales = self.excite + red * wide // mid
        self.scale_taps = mid // red
        groups = -(-2 * len(TAPS) // self.scale_taps)
        self.squeeze = self.scales + groups * red
        self.expand = self.squeeze + wide * red // mid
        self.spatial = self.expand + wide
        self.reduce = self.spatial + len(TAPS) * mid
        self.stem = self.reduce + wide
        self.rows = self.stem + LANES


def job_list(lay, mid):
    early = lay.expand - lay.excite
    jobs = [[(0, 1024, 0), (1024, early - 1024, 1)]]
    half = (lay.spatial - lay.expand) // 2
    jobs.append([(lay.expand, half, 0), (lay.expand + half, half, 1)])
    spatial, at, kind = [], lay.spatial, 0
    while at < lay.reduce:
        size = min(1024, lay.reduce - at)
        spatial.append((at, size, kind))
        at, kind = at + size, 1 - kind
    jobs.append(spatial)
    half = (lay.stem - lay.reduce) // 2
    jobs.append([(lay.reduce, half, 0), (lay.reduce + half, half, 1), (lay.stem, lay.rows - lay.stem, 0)])
    return jobs


def block_kernel(clips, segs, grid, names, sc_names, *refs):
    R = SimpleNamespace(**dict(zip(names, refs[: len(names)])))
    S = SimpleNamespace(**dict(zip(sc_names, refs[len(names) :])))
    rows, wide = S.x.shape
    mid, red = S.f1.shape[1], S.sq.shape[1]
    cells = grid * grid
    images = rows // cells
    lay = Layout(wide, mid, red)
    blocks = range(0, rows, BLOCK)
    ntap = len(TAPS)
    place = Place(clips, segs)
    local, sends, recvs = Sems(S.local), Sems(S.send), Sems(S.recv)

    wfine = S.wfc.at[pl.ds(0, ntap * red)]
    wcoarse = S.wfc.at[pl.ds(ntap * red, ntap * red)]

    def load(src, dst):
        copy = pltpu.make_async_copy(src, dst, local.take())
        copy.start()
        return copy

    loads = SimpleNamespace(
        x=load(R.x, S.x),
        frames=load(R.frames, S.frames),
        wr=load(R.wr, S.wr),
        ws=load(R.ws, S.ws),
        we=load(R.we, S.we),
        wq=load(R.wq, S.wq),
        wf=load(R.wf, wfine),
        wc=load(R.wc, wcoarse),
        wx=load(R.wx, S.wx),
        cot=load(R.cot, S.cot),
        stem_cot=load(R.stem_cot, S.stem_cot),
    )

    place.greet()

    groups = R.groups
    total_groups = groups.shape[0]

    def side_of(group):
        return 5 + 2 * group - group // 2

    def area(k, acc):
        side = side_of(groups[k])
        return acc + side * side

    count = lax.fori_loop(0, total_groups, area, jnp.int32(0)) * segs
    inv = 1.0 / jnp.full((1, LANES), count.astype(F32), F32)
    cell = lax.broadcasted_iota(jnp.int32, (cells, LANES), 0)
    ci, cj = cell // grid, lax.rem(cell, grid)
    for img in range(images):
        side = side_of(groups[place.clip * images + img])
        S.mask[img * cells : (img + 1) * cells] = jnp.where((ci < side) & (cj < side), 1.0, 0.0).astype(F32)
    half = grid // 2
    small = lax.rem(cell, half * half)
    si, sj = small // half, lax.rem(small, half)
    for t, (di, dj) in enumerate(TAPS):
        ok = (ci + di >= 0) & (ci + di < grid) & (cj + dj >= 0) & (cj + dj < grid)
        S.tap[t] = jnp.where(ok, 1.0, 0.0).astype(F32)
        ok = (si + di >= 0) & (si + di < half) & (sj + dj >= 0) & (sj + dj < half)
        S.tap_small[t] = jnp.where(ok, 1.0, 0.0).astype(F32)
    mask, tap, tap_small = S.mask, S.tap, S.tap_small
    srow = lax.broadcasted_iota(jnp.int32, (images * half * half, rows), 0)
    brow = lax.broadcasted_iota(jnp.int32, (images * half * half, rows), 1)
    parent = (brow // cells) * half * half + (lax.rem(brow, cells) // grid) // 2 * half + lax.rem(brow, grid) // 2
    S.pool[...] = jnp.where(srow == parent, 0.25, 0.0).astype(BF16)
    brow = lax.broadcasted_iota(jnp.int32, (rows, images * half * half), 0)
    srow = lax.broadcasted_iota(jnp.int32, (rows, images * half * half), 1)
    parent = (brow // cells) * half * half + (lax.rem(brow, cells) // grid) // 2 * half + lax.rem(brow, grid) // 2
    S.up[...] = jnp.where(srow == parent, 1.0, 0.0).astype(BF16)
    for ref in (S.tmp, S.z, S.tmp_small):
        ref[:PAD] = jnp.zeros((PAD, ref.shape[1]), F32)
        ref[ref.shape[0] - PAD :] = jnp.zeros((PAD, ref.shape[1]), F32)
    grads = S.grads

    near = [S.near0, S.near1, S.near2, S.near3, S.near4, S.near5]
    far = [S.far0, S.far1, S.far2, S.far3, S.far4, S.far5]
    stats = [S.res0, S.res1, S.res2, S.res3, S.res4, S.res5]

    def sums(k):
        return Sums(place, near[k], far[k], stats[k], sends, recvs)

    all_sums = [sums(k) for k in range(6)]

    def local_moments(src, width, ar, masked):
        def body(at, j):
            s = q = jnp.zeros((8, LANES), F32)
            for r in blocks:
                v = src[r : r + BLOCK, lanes(at)]
                w = v * mask[r : r + BLOCK] if masked else v
                s, q = s + fold(w), q + fold(w * v)
            ar.put(0, at, total_of(s))
            ar.put(1, at, total_of(q))

        columns(width, body)

    gains = [R.gain_one, R.gain_two, R.gain_three]
    biases = [R.bias_one, R.bias_two, R.bias_three]

    def affine(k, at):
        stat = stats[k]
        mean = stat[0:1, lanes(at)] * inv
        spread = stat[1:2, lanes(at)] * inv - mean * mean
        root = lax.rsqrt(spread + 1e-05)
        scale = root * gains[k][0:1, lanes(at)]
        return scale, biases[k][0:1, lanes(at)] - mean * scale, mean, root

    def spread_taps(tmp, masks, per, count, stride, store):
        for t, (di, dj) in enumerate(TAPS):
            off = PAD + di * stride + dj
            for r in range(0, count, BLOCK):
                v = tmp[r + off : r + off + BLOCK, :] * masks[t, r % per : r % per + BLOCK]
                store(t, r, v)

    def gather_taps(z, width, masks, per, r, stride, at):
        acc = None
        for t, (di, dj) in enumerate(TAPS):
            off = PAD + r + di * stride + dj
            v = z[off : off + BLOCK, lanes((ntap - 1 - t) * width + at)] * masks[t, r % per : r % per + BLOCK]
            acc = v if acc is None else acc + v
        return acc

    stem = Stem(R, S, images, S.frames.shape[1], float(S.stem_cot.shape[0] * clips * segs))
    loads.x.wait()
    x = S.x

    def cut(at, j):
        for r in blocks:
            x[r : r + BLOCK, lanes(at)] = (x[r : r + BLOCK, lanes(at)].astype(F32) * mask[r : r + BLOCK]).astype(BF16)

    columns(wide, cut)
    loads.wr.wait()
    S.f1[...] = dot(x[...], S.wr[...])
    local_moments(S.f1, mid, all_sums[0], False)
    all_sums[0].start()
    stem.tables()
    all_sums[0].middle()
    loads.frames.wait()
    stem.patches()
    all_sums[0].finish()

    def hidden_one(at, j):
        scale, shift, _, _ = affine(0, at)
        for r in blocks:
            y = S.f1[r : r + BLOCK, lanes(at)] * scale + shift
            S.tmp[PAD + r : PAD + r + BLOCK, :] = y * jax.nn.sigmoid(y) * mask[r : r + BLOCK]

        def store(t, r, v):
            S.col[r : r + BLOCK, lanes(pl.multiple_of(t * mid + at, LANES))] = v.astype(BF16)

        spread_taps(S.tmp, tap, cells, rows, grid, store)

    columns(mid, hidden_one)
    loads.ws.wait()
    S.f2[...] = dot(S.col[...], S.ws[...])
    local_moments(S.f2, mid, all_sums[1], True)
    all_sums[1].start()
    stem.forward(all_sums[2], wide)
    all_sums[1].middle()
    all_sums[1].finish()

    def hidden_two(at, j):
        scale, shift, _, _ = affine(1, at)
        for r in blocks:
            y = S.f2[r : r + BLOCK, lanes(at)] * scale + shift
            S.h2[r : r + BLOCK, lanes(at)] = (y * jax.nn.sigmoid(y) * mask[r : r + BLOCK]).astype(BF16)

    columns(mid, hidden_two)
    loads.we.wait()
    S.f3[...] = dot(S.h2[...], S.we[...])
    local_moments(S.f3, wide, all_sums[2], False)
    all_sums[2].start()
    all_sums[2].middle()
    all_sums[2].finish()

    def branch_low(at, j):
        scale, shift, _, _ = affine(2, at)
        for r in blocks:
            y = (S.f3[r : r + BLOCK, lanes(at)] * scale + shift) * mask[r : r + BLOCK]
            S.branch[r : r + BLOCK, lanes(at)] = y.astype(BF16)

    columns(wide, branch_low)
    loads.wq.wait()
    S.sq[...] = dot(S.branch[...], S.wq[...]).astype(BF16)

    def swap(mine, slots):
        after, before = lax.rem(place.seg + 1, segs), lax.rem(place.seg + segs - 1, segs)
        copies = [
            remote(mine, slots.at[0], sends, recvs, (place.clip, after)),
            remote(mine, slots.at[1], sends, recvs, (place.clip, before)),
        ]
        return copies

    has_before = jnp.where(jnp.full((1, LANES), place.seg, jnp.int32) > 0, 1.0, 0.0).astype(F32)
    has_after = jnp.where(jnp.full((1, LANES), place.seg, jnp.int32) < segs - 1, 1.0, 0.0).astype(F32)
    copies = swap(S.sq, S.halo)
    for copy in copies:
        copy.wait()

    diffs = S.diffs
    for r in blocks:
        own = S.sq[r : r + BLOCK].astype(F32)
        later = S.halo[1, r : r + BLOCK].astype(F32) * has_after - own
        earlier = S.halo[0, r : r + BLOCK].astype(F32) * has_before - own
        diffs[r : r + BLOCK, lanes(0, red)] = later.astype(BF16)
        diffs[r : r + BLOCK, lanes(red, red)] = earlier.astype(BF16)
        S.tmp[PAD + r : PAD + r + BLOCK, :] = later.astype(BF16).astype(F32) + earlier.astype(BF16).astype(F32)

    def store_fine(t, r, v):
        S.cc[r : r + BLOCK, lanes(t * red, red)] = v.astype(BF16)

    spread_taps(S.tmp, tap, cells, rows, grid, store_fine)
    pooled = dot(S.pool[...], diffs[...]).astype(BF16).astype(F32)
    small_rows = pooled.shape[0]
    S.tmp_small[PAD : PAD + small_rows, :] = pooled[:, :red] + pooled[:, red:]

    def store_small(t, r, v):
        S.small_col[r : r + BLOCK, lanes(t * red, red)] = v.astype(BF16)

    spread_taps(S.tmp_small, tap_small, cells, small_rows, half, store_small)
    S.cc[:, lanes(ntap * red, ntap * red)] = dot(S.up[...], S.small_col[...]).astype(BF16)
    loads.wf.wait()
    loads.wc.wait()
    S.mo[...] = dot(S.cc[...], S.wfc[...]).astype(BF16)
    loads.wx.wait()
    S.gb[...] = dot(S.mo[...], S.wx[...])
    loads.cot.wait()

    def ends(at, j):
        scale, shift, _, _ = affine(2, at)
        for r in blocks:
            here = (slice(r, r + BLOCK), lanes(at))
            m = mask[r : r + BLOCK]
            branch = (S.f3[here] * scale + shift) * m
            gate = jax.nn.sigmoid(S.gb[here])
            z = x[here].astype(F32) + branch * (1.0 + gate)
            s = jax.nn.sigmoid(z)
            out = z * s
            gz = S.cot[here].astype(F32) * m * (s + out * (1.0 - s))
            S.cot[here] = (out * m).astype(BF16)
            S.gi[here] = gz
            S.gb[here] = gz * (1.0 + gate)
            S.g3[here] = (gz * branch * gate * (1.0 - gate)).astype(BF16)

    columns(wide, ends)
    out_copy = pltpu.make_async_copy(S.cot, R.block_out, local.take())
    out_copy.start()

    S.gm[...] = dot_bt(S.g3[...], S.wx[...]).astype(BF16)
    zf = dot_bt(S.gm[...], S.wfc[0 : ntap * red, :])
    S.z[PAD : PAD + rows, lanes(0, ntap * red)] = zf
    gmc = lax.dot_general(S.up[...], S.gm[...], (((0,), (0,)), ((), ())), preferred_element_type=F32).astype(BF16)
    S.z[PAD : PAD + small_rows, lanes(ntap * red, ntap * red)] = dot_bt(gmc, S.wfc[ntap * red :, :])
    S.z[PAD + small_rows : PAD + small_rows + PAD, lanes(ntap * red, ntap * red)] = jnp.zeros((PAD, ntap * red), F32)
    coarse = gather_taps(S.z, red, tap_small, cells, 0, half, ntap * red)
    coarse = dot_at(S.pool[...], coarse.astype(BF16))
    for r in blocks:
        gd = gather_taps(S.z, red, tap, cells, r, grid, 0) + coarse[r : r + BLOCK]
        S.gd[r : r + BLOCK] = gd
        S.gd_low[r : r + BLOCK] = gd.astype(BF16)
    copies = swap(S.gd_low, S.halo2)
    last = lay.squeeze - red
    grads[last : lay.squeeze] = jnp.zeros((red, mid), BF16)
    for b in range(wide // mid):
        grads[lay.excite + b * red : lay.excite + (b + 1) * red] = dot_at(
            S.mo[...], S.g3[:, lanes(b * mid, mid)]
        ).astype(BF16)
    for t in range(2 * ntap):
        top = lay.scales + t // lay.scale_taps * red
        grads[top : top + red, lanes(t % lay.scale_taps * red, red)] = dot_at(
            S.cc[:, lanes(t * red, red)], S.gm[...]
        ).astype(BF16)
    for copy in copies:
        copy.wait()
    for r in blocks:
        g = S.halo2[0, r : r + BLOCK].astype(F32) * has_before + S.halo2[1, r : r + BLOCK].astype(F32) * has_after
        S.gsq[r : r + BLOCK] = (g - 2.0 * S.gd[r : r + BLOCK]).astype(BF16)
    S.z[PAD : PAD + rows, lanes(0, wide)] = dot_bt(S.gsq[...], S.wq[...])

    def branch_grad(at, j):
        _, _, mean, root = affine(2, at)
        s = q = jnp.zeros((8, LANES), F32)
        for r in blocks:
            here = (slice(r, r + BLOCK), lanes(at))
            g = (S.gb[here] + S.z[PAD + r : PAD + r + BLOCK, lanes(at)]) * mask[r : r + BLOCK]
            S.gb[here] = g
            s, q = s + fold(g), q + fold(g * ((S.f3[here] - mean) * root))
        all_sums[3].put(0, at, total_of(s))
        all_sums[3].put(1, at, total_of(q))

    columns(wide, branch_grad)
    all_sums[3].start()
    loads.stem_cot.wait()
    stem.rear(stats[2][:, lanes(wide)], all_sums[4], mid)
    stem_copy = pltpu.make_async_copy(S.stem_cot, R.stem_out, local.take())
    stem_copy.start()
    for b in range(mid // red):
        grads[lay.squeeze : lay.squeeze + mid, lanes(b * red, red)] = dot_at(
            S.branch[:, lanes(b * mid, mid)], S.gsq[...]
        ).astype(BF16)
    all_sums[3].middle()
    all_sums[3].finish()

    def through(k, back, src, given, dst, width):
        stat = stats[back]

        def body(at, j):
            scale, _, mean, root = affine(k, at)
            gb, gg = stat[0:1, lanes(at)] * inv, stat[1:2, lanes(at)] * inv
            for r in blocks:
                here = (slice(r, r + BLOCK), lanes(at))
                hat = (src[here] - mean) * root
                dst[here] = (scale * (given[here] - (gb + hat * gg) * mask[r : r + BLOCK])).astype(BF16)

        columns(width, body)

    def act_back(k, ar, src, value, at):
        scale, shift, mean, root = affine(k, at)
        s = q = jnp.zeros((8, LANES), F32)
        for r in blocks:
            here = (slice(r, r + BLOCK), lanes(at))
            a = src[here]
            y = a * scale + shift
            sg = jax.nn.sigmoid(y)
            g = value(r) * mask[r : r + BLOCK] * (sg * (1.0 + y * (1.0 - sg)))
            S.gy[here] = g
            s, q = s + fold(g), q + fold(g * ((a - mean) * root))
        ar.put(0, at, total_of(s))
        ar.put(1, at, total_of(q))

    through(2, 3, S.f3, S.gb, S.g3, wide)
    S.gh[...] = dot_bt(S.g3[...], S.we[...])

    def back_two(at, j):
        act_back(1, all_sums[4], S.f2, lambda r: S.gh[r : r + BLOCK, lanes(at)], at)

    columns(mid, back_two)
    all_sums[4].start()
    for b in range(wide // mid):
        grads[lay.expand + b * mid : lay.expand + (b + 1) * mid] = dot_at(
            S.h2[...], S.g3[:, lanes(b * mid, mid)]
        ).astype(BF16)
    all_sums[4].middle()
    all_sums[4].finish()
    through(1, 4, S.f2, S.gy, S.g2, mid)
    S.z[PAD : PAD + rows, :] = dot_bt(S.g2[...], S.ws[...])

    def back_one(at, j):
        act_back(
            0,
            all_sums[5],
            S.f1,
            lambda r: gather_taps_at(S.z, mid, tap, cells, r, grid, at),
            at,
        )

    def gather_taps_at(z, width, masks, per, r, stride, at):
        acc = None
        for t, (di, dj) in enumerate(TAPS):
            off = PAD + r + di * stride + dj
            start = pl.multiple_of((ntap - 1 - t) * width + at, LANES)
            v = z[off : off + BLOCK, lanes(start)] * masks[t, r % per : r % per + BLOCK]
            acc = v if acc is None else acc + v
        return acc

    columns(mid, back_one)
    all_sums[5].start()

    def spatial_grad(t, carry):
        start = pl.multiple_of(t * mid, mid)
        grads[pl.ds(pl.multiple_of(lay.spatial + start, LANES), mid)] = dot_at(
            S.col[:, lanes(start, mid)], S.g2[...]
        ).astype(BF16)
        return carry

    lax.fori_loop(0, ntap, spatial_grad, 0)
    all_sums[5].middle()
    stem.back(stats[4][:, lanes(mid)], lay.stem)
    all_sums[5].finish()
    through(0, 5, S.f1, S.gy, S.g1, mid)
    for b in range(wide // mid):
        grads[lay.reduce + b * mid : lay.reduce + (b + 1) * mid] = dot_at(
            x[:, lanes(b * mid, mid)], S.g1[...]
        ).astype(BF16)
    S.z[PAD : PAD + rows, lanes(0, wide)] = dot_bt(S.g1[...], S.wr[...])

    def features_grad(at, j):
        for r in blocks:
            here = (slice(r, r + BLOCK), lanes(at))
            g = (S.gi[here] + S.z[PAD + r : PAD + r + BLOCK, lanes(at)]) * mask[r : r + BLOCK]
            S.g3[here] = g.astype(BF16)

    columns(wide, features_grad)
    feat_copy = pltpu.make_async_copy(S.g3, R.grad_features, local.take())
    feat_copy.start()

    jobs, land = [], 0
    for group in job_list(lay, mid):
        for base, size, kind in group:
            job = Job(
                place, grads, S.landing, R.packed, base, size, bit_order(clips, segs, kind), land, local, sends, recvs
            )
            land = job.land_end
            jobs.append(job)
    for job in jobs:
        job.scatter_start()
    count_steps = len(jobs[0].steps)
    for k in range(count_steps):
        for job in jobs:
            job.scatter_finish()
            if k + 1 < count_steps:
                job.scatter_start()
            else:
                job.own_start()
    for job in jobs:
        job.own_finish()
        job.gather_start()
    for k in range(count_steps):
        for job in jobs:
            job.gather_finish()
            if k + 1 < count_steps:
                job.gather_start()
    small = R.sums
    at = 0
    for k, width in ((5, mid), (4, mid + LANES), (3, wide)):
        small[:, lanes(at, width)] = stats[k][...]
        at += width
    stem_copy.wait()
    out_copy.wait()
    feat_copy.wait()


def block(clips, segs, feats, cot, res_group, deep, stem):
    (w_reduce, gain_one, bias_one, w_spatial, gain_two, bias_two, w_expand, gain_three, bias_three) = deep[:9]
    w_squeeze, w_fine, w_coarse, w_excite = deep[9:]
    images, _, grid, _, wide = feats.shape
    rows = images * grid * grid
    mid, red = w_reduce.shape[1], w_squeeze.shape[1]
    taps = len(TAPS)
    lay = Layout(wide, mid, red)
    small_rows = rows // 4
    frames, stem_cot, stem_weight, diff_weight, stem_gain, stem_bias = stem
    count, side, colours = frames.shape[2], frames.shape[3], frames.shape[5]
    kernel, channels = stem_weight.shape[0], stem_weight.shape[3]
    stem_cells = images * (side // 2) ** 2
    stem_rows = images * side // 2
    stem_lanes = side // 2 * channels
    depth = colours * side * 8 + 3 * 256
    inputs = dict(
        x=feats.reshape(rows, wide),
        cot=cot.reshape(rows, wide),
        groups=res_group,
        wr=w_reduce,
        ws=w_spatial.reshape(taps * mid, mid),
        we=w_expand,
        wq=w_squeeze,
        wf=w_fine.reshape(taps * red, red),
        wc=w_coarse.reshape(taps * red, red),
        wx=w_excite,
        gain_one=gain_one.reshape(1, mid),
        bias_one=bias_one.reshape(1, mid),
        gain_two=gain_two.reshape(1, mid),
        bias_two=bias_two.reshape(1, mid),
        gain_three=gain_three.reshape(1, wide),
        bias_three=bias_three.reshape(1, wide),
        frames=jnp.transpose(frames, (0, 1, 2, 5, 3, 4)).reshape(images * count * colours, side, side),
        stem_cot=stem_cot.reshape(stem_cells, channels),
        stem_w=jnp.transpose(stem_weight, (0, 2, 1, 3)).reshape(kernel * colours, kernel, channels),
        diff_w=diff_weight.reshape(len(TAPS), diff_weight.shape[2], channels),
        stem_gain=stem_gain.reshape(1, channels),
        stem_bias=stem_bias.reshape(1, channels),
    )
    outputs = dict(
        block_out=jax.ShapeDtypeStruct((rows, wide), BF16),
        grad_features=jax.ShapeDtypeStruct((rows, wide), BF16),
        packed=jax.ShapeDtypeStruct((lay.rows, mid), BF16),
        sums=jax.ShapeDtypeStruct((2, 2 * mid + wide + LANES), F32),
        stem_out=jax.ShapeDtypeStruct((stem_cells, channels), BF16),
    )

    def spec(name):
        if name == "groups":
            return pl.BlockSpec(memory_space=pltpu.SMEM)
        if inputs.get(name, frames).size < 1 << 15 or name == "sums":
            return pl.BlockSpec(memory_space=pltpu.VMEM)
        return pl.BlockSpec(memory_space=pl.ANY)

    jobs = [job for group in job_list(lay, mid) for job in group]
    land = sum(landing_rows(size, bit_order(clips, segs, kind)) for _, size, kind in jobs)
    bits = len(bit_order(clips, segs, 0))
    near, far = 2 * segs, clips // 2
    remote_count = len(jobs) * bits * 2 + 6 * (near + far) + 8
    v = pltpu.VMEM
    scratch = dict(
        x=v((rows, wide), BF16),
        cot=v((rows, wide), BF16),
        wr=v((wide, mid), BF16),
        ws=v((taps * mid, mid), BF16),
        we=v((mid, wide), BF16),
        wq=v((wide, red), BF16),
        wfc=v((2 * taps * red, red), BF16),
        wx=v((red, wide), BF16),
        mask=v((rows, LANES), F32),
        tap=v((taps, grid * grid, LANES), F32),
        tap_small=v((taps, grid * grid, LANES), F32),
        pool=v((small_rows, rows), BF16),
        up=v((rows, small_rows), BF16),
        tmp=v((rows + 2 * PAD, LANES), F32),
        tmp_small=v((small_rows + 2 * PAD, LANES), F32),
        small_col=v((small_rows, taps * red), BF16),
        f1=v((rows, mid), F32),
        f2=v((rows, mid), F32),
        f3=v((rows, wide), F32),
        col=v((rows, taps * mid), BF16),
        h2=v((rows, mid), BF16),
        branch=v((rows, wide), BF16),
        sq=v((rows, red), BF16),
        halo=v((2, rows, red), BF16),
        halo2=v((2, rows, red), BF16),
        diffs=v((rows, 2 * red), BF16),
        cc=v((rows, 2 * taps * red), BF16),
        mo=v((rows, red), BF16),
        gm=v((rows, red), BF16),
        gd=v((rows, red), F32),
        gd_low=v((rows, red), BF16),
        gsq=v((rows, red), BF16),
        gb=v((rows, wide), F32),
        gi=v((rows, wide), F32),
        g3=v((rows, wide), BF16),
        gh=v((rows, mid), F32),
        gy=v((rows, mid), F32),
        g2=v((rows, mid), BF16),
        g1=v((rows, mid), BF16),
        z=v((rows + 2 * PAD, taps * mid), F32),
        grads=v((lay.rows, mid), BF16),
        landing=v((land, mid), BF16),
        frames=v((images * count * colours, side, side), BF16),
        stem_cot=v((stem_cells, channels), BF16),
        stem_wide=v((stem_cells, LANES), F32),
        stem_stat=v((2, LANES), F32),
        padded=v((images * (side + 8), LANES), F32),
        stem_taps=v((stem_rows, 512), F32),
        columns=v((2, images * side, LANES), F32),
        xx=v((stem_rows, depth), BF16),
        pre=v((stem_rows, stem_lanes), F32),
        gpre=v((stem_rows, stem_lanes), F32),
        prod=v((depth, LANES), F32),
        bands=v((240, LANES), F32),
        spots=v((144, LANES), F32),
        wt=v((192, LANES), F32),
        wd=v((144, LANES), F32),
    )
    for k, width in enumerate((mid, mid, wide + LANES, wide, mid + LANES, mid)):
        scratch[f"near{k}"] = v((near, 2, width), F32)
        scratch[f"far{k}"] = v((far, 2, width), F32)
        scratch[f"res{k}"] = v((2, width), F32)
    scratch.update(
        local=pltpu.SemaphoreType.DMA((32,)),
        send=pltpu.SemaphoreType.DMA((remote_count,)),
        recv=pltpu.SemaphoreType.DMA((remote_count,)),
    )
    names = list(inputs) + list(outputs)
    result = pl.pallas_call(
        partial(block_kernel, clips, segs, grid, names, list(scratch)),
        out_shape=list(outputs.values()),
        in_specs=[spec(name) for name in inputs],
        out_specs=[spec(name) for name in outputs],
        scratch_shapes=list(scratch.values()),
        compiler_params=pltpu.CompilerParams(
            collective_id=0, has_side_effects=True, vmem_limit_bytes=VMEM_LIMIT
        ),
        name="block",
    )(*inputs.values())
    return result


VMEM_LIMIT = 62 << 20


def spread_kernel(lay, mid, red, wide, packed, reduce, spatial, expand, squeeze, fine, coarse, excite, stem, held, wide_held, reads, writes):
    taps = len(TAPS)
    parts = []
    at = 0
    while at < lay.rows:
        size = min(512, lay.rows - at)
        if at < lay.expand:
            size = {lay.excite: lay.scales - lay.excite, lay.scales: lay.squeeze - lay.scales, lay.squeeze: lay.expand - lay.squeeze}[at]
        parts.append((at, size))
        at += size
    copies = []
    for k, (at, size) in enumerate(parts):
        copy = pltpu.make_async_copy(packed.at[pl.ds(at, size)], held.at[pl.ds(at, size)], reads.at[k])
        copy.start()
        copies.append(copy)
    out, used = [], 0

    def write(src, dst):
        copy = pltpu.make_async_copy(src, dst, writes.at[len(out)])
        copy.start()
        out.append(copy)

    for k, (at, size) in enumerate(parts):
        copies[k].wait()

        def convert(i, carry):
            here = pl.ds(pl.multiple_of(at + i * 32, 32), 32)
            wide_held[here] = held[here].astype(F32)
            return carry

        lax.fori_loop(0, size // 32, convert, 0)
        block = wide_held.at[pl.ds(at, size)]
        if at == lay.excite:
            for b in range(wide // mid):
                write(wide_held.at[pl.ds(at + b * red, red)], excite.at[:, pl.ds(b * mid, mid)])
        elif at == lay.scales:
            for t in range(2 * taps):
                src = wide_held.at[
                    pl.ds(at + t // lay.scale_taps * red, red), pl.ds(t % lay.scale_taps * red, red)
                ]
                dst = fine if t < taps else coarse
                write(src, dst.at[pl.ds(t % taps * red, red)])
        elif at == lay.squeeze:
            for b in range(mid // red):
                write(wide_held.at[pl.ds(at, mid), pl.ds(b * red, red)], squeeze.at[pl.ds(b * mid, mid)])
        elif at == lay.stem:
            write(block, stem)
        elif at < lay.spatial:
            write(block, expand.at[:, pl.ds(at - lay.expand, size)])
        elif at < lay.reduce:
            write(block, spatial.at[pl.ds(at - lay.spatial, size)])
        else:
            write(block, reduce.at[pl.ds(at - lay.reduce, size)])
    for copy in out:
        copy.wait()


def spread(packed, mid, red, wide):
    lay = Layout(wide, mid, red)
    taps = len(TAPS)
    shapes = [(wide, mid), (taps * mid, mid), (mid, wide), (wide, red), (taps * red, red), (taps * red, red), (red, wide), (LANES, mid)]
    return pl.pallas_call(
        partial(spread_kernel, lay, mid, red, wide),
        out_shape=[jax.ShapeDtypeStruct(shape, F32) for shape in shapes],
        in_specs=[pl.BlockSpec(memory_space=pl.ANY)],
        out_specs=[pl.BlockSpec(memory_space=pl.ANY)] * len(shapes),
        scratch_shapes=[
            pltpu.VMEM((lay.rows, mid), BF16),
            pltpu.VMEM((lay.rows, mid), F32),
            pltpu.SemaphoreType.DMA((64,)),
            pltpu.SemaphoreType.DMA((64,)),
        ],
        compiler_params=pltpu.CompilerParams(vmem_limit_bytes=VMEM_LIMIT),
        name="spread",
    )(packed)


def shards(
    frames,
    features,
    res_group,
    stem_weight,
    diff_weight,
    stem_gain,
    stem_bias,
    w_reduce,
    gain_one,
    bias_one,
    w_spatial,
    gain_two,
    bias_two,
    w_expand,
    gain_three,
    bias_three,
    w_squeeze,
    w_fine,
    w_coarse,
    w_excite,
    stem_cotangent,
    block_cotangent,
):
    clips, segs = lax.axis_size("clip"), lax.axis_size("seg")
    wide, mid, red = w_reduce.shape[0], w_reduce.shape[1], w_squeeze.shape[1]
    deep = (
        w_reduce, gain_one, bias_one, w_spatial, gain_two, bias_two, w_expand, gain_three, bias_three,
        w_squeeze, w_fine, w_coarse, w_excite,
    )
    stem = (frames, stem_cotangent, stem_weight, diff_weight, stem_gain, stem_bias)
    block_out, grad_feats, packed, sums, stem_out = block(
        clips, segs, features, block_cotangent, res_group, deep, stem
    )
    g_reduce, g_spatial, g_expand, g_squeeze, g_fine, g_coarse, g_excite, g_stem = spread(packed, mid, red, wide)
    kernel, colours, channels = stem_weight.shape[0], stem_weight.shape[2], stem_weight.shape[3]
    parts = [g_stem[:, k * LANES : k * LANES + channels] for k in range(4)]
    g_stem_w = jnp.concatenate(parts[:2])[: colours * kernel * 8].reshape(colours, kernel, 8, channels)
    g_stem_w = jnp.transpose(g_stem_w[:, :, :kernel], (2, 1, 0, 3))
    g_diff_w = jnp.concatenate([parts[2], parts[3][:16]]).reshape(3, 3, 16, channels)[:, :, : diff_weight.shape[2]]

    def pick(row, at, width):
        return sums[row, at : at + width]

    return (
        stem_out.reshape(stem_cotangent.shape),
        block_out.reshape(features.shape),
        grad_feats.reshape(features.shape),
        g_stem_w,
        g_diff_w,
        pick(1, 2 * mid, channels),
        pick(0, 2 * mid, channels),
        g_reduce,
        pick(1, 0, mid),
        pick(0, 0, mid),
        g_spatial.reshape(w_spatial.shape),
        pick(1, mid, mid),
        pick(0, mid, mid),
        g_expand,
        pick(1, 2 * mid + LANES, wide),
        pick(0, 2 * mid + LANES, wide),
        g_squeeze,
        g_fine.reshape(w_fine.shape),
        g_coarse.reshape(w_coarse.shape),
        g_excite,
    )


def solution(mesh):
    split = P("clip", "seg")
    whole = P()
    ins = (split, split) + (whole,) * 18 + (split, split)
    outs = (split,) * 3 + (whole,) * 17
    return jax.shard_map(shards, mesh=mesh, in_specs=ins, out_specs=outs, check_vma=False)
```

time: 1040 us -> 232 us (0.22); the launches traced: 1020 us -> 231 us
  blocking collectives: 473 us -> 0 us
  local copies, waits for them, and re-layouts: 327 us -> 9.13 us
  Pallas kernels: 0 us -> 221 us
  waiting for transfers between devices: 82.2 us -> 0 us
  matrix products: 64.2 us -> 0 us
  other arithmetic: 43.7 us -> 0.65 us
  starting transfers between devices: 16.2 us -> 0 us
  between operations: 16.5 us -> 0.7 us
    psum x6 -> x0, blocking collectives: 245 us -> none  [the longest x4 163 us: synced(): return (lax.psum(local_sums, ('clip', 'seg')), pull_sums)]
    unnamed x1 -> x0, blocking collectives: 228 us -> none
    pallas_call x0 -> x2, Pallas kernels: none -> 221 us  [the longest x1 209 us: block(): pl.pallas_call(partial(block_kernel, clips, segs, grid, names, list(scrat...]
    concatenate x1 -> x0, local copies, waits for them, and re-layouts: 183 us -> none  [pack_grads(): flat = jnp.concatenate([grad.reshape(-1) for grad in grads])]
    all_gather x1 -> x0, waiting for transfers between devices: 82.1 us -> none  [shards(): lax.all_gather(shares.astype(jnp.bfloat16), ('clip', 'seg'), axis=0, tile...]
    reshape x11 -> x0, local copies, waits for them, and re-layouts: 62.4 us -> none  [the longest x6 23.1 us: unpack_grads(): pieces.append(flat[offset:offset + grad.size].reshape(grad.shape))]
    conv_general_dilated x17 -> x0, matrix products: 36.7 us -> none  [convolve(): lax.conv_general_dilated(image, kernel, (stride, stride), 'SAME', dimensi...]
    unnamed x212 -> x10, local copies, waits for them, and re-layouts: 33.3 us -> 3.42 us
  transfers between devices with their start and end apart: 6 -> 0, of which waited for: 2 -> 0; matrix products, arithmetic and copies ran while one was open for 6% -> 0% of each run, Pallas kernels for 0% -> 0%
where the time goes in v1:
time: 232 us; the launch traced here: 231 us
  Pallas kernels  221 us (95%)
  local copies, waits for them, and re-layouts  9.13 us (4%)
    pallas_call x1, Pallas kernels, block(): pl.pallas_call(partial(block_kernel, clips, segs, grid, names, list(scrat...  209 us
    pallas_call x1, Pallas kernels, spread(): pl.pallas_call(partial(spread_kernel, lay, mid, red, wide), out_shape=[ja...  11.8 us

profile of v1, /device:TPU:0, one launch (start us, length us, event | category | flops | bytes accessed | tf_op | source)
XLA Modules:
  0.0 231.2 jit_solution(410222601358984644)
XLA Ops:
  0.7 208.9 %block.1 = (bf16[256,2048]{1,0:T(8,128)(2,1)}, bf16[256,2048]{1,0:T(8,128)(2,1)}, bf16[10496,512]{1,0:T(8,128)(2,1)}, f32[2,3200]{1,0:T(2,128)}, bf16[2304,64]{1,0:T(8,128)(2,1)}) custom-call(bf16[256,2048]{1,0:T(8,128)(2,1)} %bitcast.51, bf16[256,2048]{1,0:T(8,128)(2,1)} %bitcast.52, s32[32]{0:T(128)} %refs_2_.1, bf16[2048,512]{1,0:T(8,128)(2,1)} %refs_3_.1, ...), custom_call_target="tpu_custom_call" | custom-call | tf_op jit(solution)/shard_map/block/pallas_call | solution.py:1052
  209.5 1.3 slice_bitcast_fusion
  210.8 1.3 fusion.2
  212.1 1.4 fusion.1
  213.6 0.0 copy-start.2
  213.6 0.0 copy-start.1
  213.6 11.8 %spread.1 = (f32[2048,512]{1,0:T(8,128)}, f32[4608,512]{1,0:T(8,128)}, f32[512,2048]{1,0:T(8,128)}, f32[2048,128]{1,0:T(8,128)}, f32[1152,128]{1,0:T(8,128)}, /*...) custom-call(bf16[10496,512]{1,0:T(8,128)(2,1)} %get-tuple-element.36.packed), custom_call_target="tpu_custom_call" | custom-call | tf_op jit(solution)/shard_map/spread/pallas_call | solution.py:1130
  225.4 0.0 copy-start
  225.4 0.8 slice.52
  226.2 0.9 fusion
  227.1 0.6 pad_maximum_fusion.1
  227.8 0.7 copy.48
  228.4 0.0 copy-done.2
  228.4 0.8 copy.52
  229.2 0.0 copy-done.1
  229.2 1.0 copy.53
  230.2 0.0 copy-done
  230.2 1.0 copy.54
  (1 shorter events, 0.0 us)
Async XLA Ops:
  213.6 14.9 %copy-start.2 = (bf16[2304,64]{1,0:T(8,128)(2,1)S(1)}, bf16[2304,64]{1,0:T(8,128)(2,1)}, u32[]{:S(2)}) copy-start(bf16[2304,64]{1,0:T(8,128)(2,1)} %get-tuple-element.33) | copy-start | bytes 884740
  213.6 15.7 %copy-start.1 = (bf16[256,2048]{1,0:T(8,128)(2,1)S(1)}, bf16[256,2048]{1,0:T(8,128)(2,1)}, u32[]{:S(2)}) copy-start(bf16[256,2048]{1,0:T(8,128)(2,1)} %get-tuple-element.34) | copy-start | bytes 3145732
  225.4 4.8 %copy-start = (bf16[256,2048]{1,0:T(8,128)(2,1)S(1)}, bf16[256,2048]{1,0:T(8,128)(2,1)}, u32[]{:S(2)}) copy-start(bf16[256,2048]{1,0:T(8,128)(2,1)} %get-tuple-element.35) | copy-start | bytes 3145732

commit v2 on v1

--- a/solution.py
+++ b/solution.py
@@ -66,6 +66,12 @@
         self.near_me = lax.rem(self.clip, 2) * segs + self.seg
         self.far_me = self.clip // 2
 
+        self.plane = 8
+        self.plane_me = lax.rem(self.clip, 2) * 4 + lax.rem(self.seg, 4)
+
+    def plane_device(self, t):
+        return ((self.clip // 2) * 2 + t // 4, (self.seg // 4) * 4 + lax.rem(t, 4))
+
     def near_device(self, t):
         return ((self.clip // 2) * 2 + t // self.segs, lax.rem(t, self.segs))
 
@@ -95,7 +101,9 @@
 
         lax.fori_loop(1, self.near, near, 0)
         lax.fori_loop(1, self.far, far, 0)
-        pl.semaphore_wait(sem, self.near + self.far - 2)
+
+    def greeted(self):
+        pl.semaphore_wait(pltpu.get_barrier_semaphore(), self.near + self.far - 2)
 
 
 def remote(src, dst, sends, recvs, device):
@@ -146,92 +154,140 @@
         self.result[...] = self._add(self.far_buf, self.place.far)
 
 
-def bit_order(clips, segs, kind):
+def bit_order(clips, segs, letters):
     seg = [("seg", 1 << k) for k in range(segs.bit_length() - 1)]
     clip = [("clip", 1 << k) for k in range(clips.bit_length() - 1)]
-    if kind == 0:
-        return seg[:1] + clip[:1] + seg[1:] + clip[1:]
-    return seg + clip
-
-
-def halvings(rows, order):
-    steps = []
-    for _ in order:
-        half = rows // 2
-        if rows % 2 == 0 and half % 16 == 0:
-            steps.append((rows, half, True))
-            rows = half
-        else:
-            steps.append((rows, rows, False))
-    return steps
+    others = seg[2:] + clip[1:]
+    named = dict(c=seg[:1], x=clip[:1], y=seg[1:2], p=others[:-1], q=others[-1:])
+    return [bit for letter in letters for bit in named[letter]]
+
+
+class Plan:
+    def __init__(self, clips, segs, first, rows, letters, nest, skip=""):
+        self.first, self.rows = first, rows
+        skip = bit_order(clips, segs, skip)
+        held = rows >> len(skip)
+        self.block, self.sums, split = held, [], list(skip)
+        for bit in bit_order(clips, segs, letters):
+            if bit in skip:
+                continue
+            half = held // 2
+            halved = held % 2 == 0 and half % 16 == 0
+            held = half if halved else held
+            self.sums.append((bit, held, halved))
+            if halved:
+                split.append(bit)
+        self.piece = held
+        self.places, size = [], rows
+        for bit in bit_order(clips, segs, nest):
+            if bit in split:
+                size //= 2
+                self.places.append((bit, size))
+        self.landing_rows = sum(size for _, size, _ in self.sums)
+        self.transfers = len(self.sums) + len(self.places)
+
+    def pieces(self):
+        bits = [bit for bit, _ in self.places]
+
+        def bits_of(number):
+            return {bit: lax.rem(lax.shift_right_logical(number, k), 2) for k, bit in enumerate(bits)}
+
+        return 1 << len(bits), bits_of
+
+    def packed_at(self, values):
+        return sum((values[bit] * size for bit, size in self.places), self.first)
+
+    def summed_at(self, values):
+        return sum((values[bit] * size for bit, size, halved in self.sums if halved), 0)
 
 
 class Job:
-    def __init__(self, place, grads, landing, packed, base, rows, order, land, local, sends, recvs):
-        self.grads, self.landing, self.packed = grads, landing, packed
-        self.local, self.sends, self.recvs = local, sends, recvs
-        self.steps = []
-        at = base
-        for (axis, stride), (size, sent, halved) in zip(order, halvings(rows, order)):
+    def __init__(self, place, plan, buffers, held, land, sems):
+        self.grads, self.landing, self.packed = buffers
+        self.local, self.sends, self.recvs = sems
+        self.sums, self.places = [], []
+        for (axis, stride), size, halved in plan.sums:
             bit, device = place.bit(axis, stride)
+            away = held
             if halved:
-                keep, away = at + bit * sent, at + (1 - bit) * sent
-            else:
-                keep, away = at, at
-            self.steps.append((keep, away, sent, halved, device, land))
-            land += sent
-            at = keep
-        self.land_end = land
-        self.at = 0
+                away = held + (1 - bit) * size
+                held = held + bit * size
+            self.sums.append((held, away, size, device, land))
+            land += size
+        self.held, self.piece, self.land_end = held, plan.piece, land
+        first = plan.first
+        for (axis, stride), size in plan.places:
+            bit, device = place.bit(axis, stride)
+            first = first + bit * size
+            self.places.append((first, size, device))
+        self.first = first
+        self.at = self.phase = 0
 
     def _rows(self, ref, start, size):
-        return ref.at[pl.ds(pl.multiple_of(start, 16), size)]
+        if not isinstance(start, int):
+            start = pl.multiple_of(start, 16)
+        return ref.at[pl.ds(start, size)]
 
     def scatter_start(self):
-        keep, away, size, halved, device, land = self.steps[self.at]
+        held, away, size, device, land = self.sums[self.at]
         self.copy = remote(
             self._rows(self.grads, away, size), self._rows(self.landing, land, size), self.sends, self.recvs, device
         )
 
     def scatter_finish(self):
-        keep, away, size, halved, device, land = self.steps[self.at]
+        held, away, size, device, land = self.sums[self.at]
         self.copy.wait()
         block = 32 if size % 32 == 0 else 16
 
         def add(k, carry):
-            mine = pl.ds(pl.multiple_of(keep + k * block, 16), block)
+            mine = pl.ds(pl.multiple_of(held + k * block, 16), block)
             theirs = pl.ds(pl.multiple_of(land + k * block, 16), block)
-            self.grads[mine] = (self.grads[mine].astype(F32) + self.landing[theirs].astype(F32)).astype(BF16)
+            self.grads[mine] = self.grads[mine] + self.landing[theirs]
             return carry
 
         lax.fori_loop(0, size // block, add, 0)
         self.at += 1
 
     def own_start(self):
-        keep, away, size, halved, device, land = self.steps[-1]
         self.copy = pltpu.make_async_copy(
-            self._rows(self.grads, keep, size), self._rows(self.packed, keep, size), self.local.take()
+            self._rows(self.grads, self.held, self.piece),
+            self._rows(self.packed, self.first, self.piece),
+            self.local.take(),
         )
         self.copy.start()
-
-    def own_finish(self):
-        self.copy.wait()
+        self.at = len(self.places)
 
     def gather_start(self):
-        keep, away, size, halved, device, land = self.steps[self.at - 1]
-        self.copy = None
-        if halved:
-            mine = self._rows(self.packed, keep, size)
-            self.copy = remote(mine, mine, self.sends, self.recvs, device)
+        first, size, device = self.places[self.at - 1]
+        mine = self._rows(self.packed, first, size)
+        self.copy = remote(mine, mine, self.sends, self.recvs, device)
 
     def gather_finish(self):
         self.at -= 1
-        if self.copy is not None:
+        self.copy.wait()
+
+    def step(self):
+        if self.phase == 0:
+            self.scatter_start()
+            self.phase = 1
+        elif self.phase == 1:
+            self.scatter_finish()
+            if self.at < len(self.sums):
+                self.scatter_start()
+            else:
+                self.own_start()
+                self.phase = 2
+        elif self.phase == 2:
             self.copy.wait()
-
-
-def landing_rows(rows, order):
-    return sum(sent for _, sent, _ in halvings(rows, order))
+            self.gather_start()
+            self.phase = 3
+        elif self.phase == 3:
+            self.gather_finish()
+            if self.at > 0:
+                self.gather_start()
+            else:
+                self.phase = 4
+        return self.phase
 
 
 class Stem:
@@ -250,19 +306,24 @@
 
     def _table(self, q):
         per = self.S.grads.shape[1] // LANES
-        return q // per * self.depth, lanes(q % per * LANES)
+        table, top = self._part(q // per)
+        return table, top, lanes(q % per * LANES)
+
+    def _part(self, n):
+        return (self.S.grads, n * self.depth) if n < 2 else (self.S.landing, 0)
 
     def tables(self):
         R, S = self.R, self.S
-        table, wt, wd = S.grads, S.wt, S.wd
+        wt, wd = S.wt, S.wd
         tall = 32
-        used = self.depth * self.pairs * LANES // table.shape[1]
 
         def clear(k, carry):
-            table[pl.ds(pl.multiple_of(k * tall, tall), tall)] = jnp.zeros((tall, table.shape[1]), BF16)
+            for n in range(3):
+                table, top = self._part(n)
+                table[pl.ds(pl.multiple_of(top + k * tall, tall), tall)] = jnp.zeros((tall, table.shape[1]), BF16)
             return carry
 
-        lax.fori_loop(0, used // tall, clear, 0)
+        lax.fori_loop(0, self.depth // tall, clear, 0)
         wt[...] = jnp.zeros(wt.shape, F32)
         wd[...] = jnp.zeros(wd.shape, F32)
         weights = R.stem_w[...].astype(F32)
@@ -283,7 +344,7 @@
                 for q in range(self.pairs):
                     j = 4 * q - 2 + 2 * p
                     if 0 <= j < self.side:
-                        top, at = self._table(q)
+                        table, top, at = self._table(q)
                         top = top + c * self.band + j * 8
                         table[top : top + 16, at] = block
         weights = R.diff_w[...].astype(F32)
@@ -296,7 +357,7 @@
                 for q in range(self.pairs):
                     j = q + kj - 1
                     if 0 <= j < self.pairs:
-                        top, at = self._table(q)
+                        table, top, at = self._table(q)
                         top = top + self.fine + ki * self.spread + j * 16
                         table[top : top + 16, at] = block
 
@@ -361,7 +422,8 @@
     def forward(self, sums, at):
         S, per = self.S, self.S.grads.shape[1]
         for n in range(self.pairs * LANES // per):
-            S.pre[:, lanes(n * per, per)] = dot(S.xx[...], S.grads[n * self.depth : (n + 1) * self.depth, :])
+            table, top = self._part(n)
+            S.pre[:, lanes(n * per, per)] = dot(S.xx[...], table[top : top + self.depth, :])
         s = q = jnp.zeros((8, LANES), F32)
         for k in range(self.pairs):
             v = S.pre[:, lanes(k * LANES)]
@@ -458,32 +520,73 @@
 
 class Layout:
     def __init__(self, wide, mid, red):
+        taps = len(TAPS)
         self.excite = 0
         self.scales = self.excite + red * wide // mid
         self.scale_taps = mid // red
-        groups = -(-2 * len(TAPS) // self.scale_taps)
+        groups = -(-2 * taps // self.scale_taps)
         self.squeeze = self.scales + groups * red
-        self.expand = self.squeeze + wide * red // mid
-        self.spatial = self.expand + wide
-        self.reduce = self.spatial + len(TAPS) * mid
-        self.stem = self.reduce + wide
-        self.rows = self.stem + LANES
-
-
-def job_list(lay, mid):
-    early = lay.expand - lay.excite
-    jobs = [[(0, 1024, 0), (1024, early - 1024, 1)]]
-    half = (lay.spatial - lay.expand) // 2
-    jobs.append([(lay.expand, half, 0), (lay.expand + half, half, 1)])
-    spatial, at, kind = [], lay.spatial, 0
-    while at < lay.reduce:
-        size = min(1024, lay.reduce - at)
-        spatial.append((at, size, kind))
-        at, kind = at + size, 1 - kind
-    jobs.append(spatial)
-    half = (lay.stem - lay.reduce) // 2
-    jobs.append([(lay.reduce, half, 0), (lay.reduce + half, half, 1), (lay.stem, lay.rows - lay.stem, 0)])
-    return jobs
+        self.stem = self.squeeze + wide * red // mid
+        self.expand = self.stem + LANES
+        self.reduce = self.expand + wide
+        self.rows = self.reduce + wide
+        self.spatial_in = mid // 2
+        self.spatial_block = taps * self.spatial_in
+        self.share_rows = 8 * self.spatial_block
+
+    def plans(self, clips, segs):
+        quarter = (self.reduce - self.expand) // 4
+        half = (self.rows - self.reduce) // 2
+
+        def plan(first, end, letters, nest):
+            return Plan(clips, segs, first, end - first, letters, nest)
+
+        cut = self.expand // 512 * 512
+        bounds = [0, cut - 512, cut, self.expand]
+        early = [plan(bounds[k], bounds[k + 1], *orders) for k, orders in enumerate(EARLY)]
+        middle = [
+            plan(self.expand + k * quarter, self.expand + (k + 1) * quarter, *orders)
+            for k, orders in enumerate(MIDDLE)
+        ]
+        late = [plan(self.reduce, self.reduce + half, *LATE[0]), plan(self.reduce + half, self.rows, *LATE[1])]
+        return early, middle, late
+
+    def shared_plans(self, clips, segs):
+        parts, first = [], 0
+        for k, nest in enumerate(SPATIAL):
+            count = min(2, len(TAPS) - 2 * k)
+            rows = 8 * count * self.spatial_in
+            parts.append((2 * k, count, Plan(clips, segs, first, rows, "cxypq", nest, "cxy")))
+            first += rows
+        return parts
+
+
+EARLY = (("cxypq", "cxypq"), ("cpyxq", "cyxpq"), ("cyxpq", "cpxqy"))
+MIDDLE = (("cpxqy", "cpyxq"), ("cpxyq", "cpxqy"), ("cpqyx", "cxypq"), ("cxypq", "cxpyq"))
+SPATIAL = ("cxypq", "cypqx", "cyxpq", "cpxqy", "cpqyx")
+LATE = (("cyxpq", "cyxpq"), ("cyxpq", "cxpqy"))
+SLOTS = (
+    (0, 1),
+    (0, 1),
+    (),
+    (),
+    (3, 4, 5, 6, 1),
+    (3, 4, 5, 6, 0, 1, 2),
+    (),
+    (),
+    (3, 2),
+    (4, 6, 0, 1),
+    (5,),
+    (12, 13, 0),
+    (7, 3, 1, 2),
+    (12, 13, 8, 4, 5, 6, 0, 1, 2),
+    (7, 9, 3, 0),
+    (8, 10, 6, 1, 2),
+    (7, 9, 11),
+    (12, 7, 0),
+    (8, 10, 6, 1),
+    (8, 2, 6, 13, 11, 4, 12, 9, 2, 3, 7, 0, 1, 9, 3, 5, 8, 10, 2, 6, 10, 12, 11, 13, 4, 5, 7, 2, 0, 4, 5, 11, 9, 3, 1, 6, 13, 10, 8, 1, 2, 12, 5, 7, 9, 12, 4, 0, 2, 11, 6, 3, 13, 0, 11, 13, 3, 10, 8, 5, 13, 7, 12, 4, 9, 7, 3, 11, 6, 8, 3, 12, 5, 13, 10, 6, 8, 4, 11, 12, 11, 13, 9, 5, 9, 5, 10, 12, 13, 4, 10, 12, 13, 4),
+)
 
 
 def block_kernel(clips, segs, grid, names, sc_names, *refs):
@@ -557,7 +660,7 @@
     srow = lax.broadcasted_iota(jnp.int32, (rows, images * half * half), 1)
     parent = (brow // cells) * half * half + (lax.rem(brow, cells) // grid) // 2 * half + lax.rem(brow, grid) // 2
     S.up[...] = jnp.where(srow == parent, 1.0, 0.0).astype(BF16)
-    for ref in (S.tmp, S.z, S.tmp_small):
+    for ref in (S.tmp, S.z, S.tmp_small, S.h1_all):
         ref[:PAD] = jnp.zeros((PAD, ref.shape[1]), F32)
         ref[ref.shape[0] - PAD :] = jnp.zeros((PAD, ref.shape[1]), F32)
     grads = S.grads
@@ -610,6 +713,33 @@
         return acc
 
     stem = Stem(R, S, images, S.frames.shape[1], float(S.stem_cot.shape[0] * clips * segs))
+    sems = (local, sends, recvs)
+    jobs, land = [], 0
+    for plan in [plan for group in lay.plans(clips, segs) for plan in group]:
+        job = Job(place, plan, (grads, S.landing, R.packed), plan.first, land, sems)
+        land = job.land_end
+        jobs.append(job)
+    shared, land, held = [], 0, 0
+    for _, _, plan in lay.shared_plans(clips, segs):
+        job = Job(place, plan, (S.shares, S.share_landing, R.shared), held, land, sems)
+        land, held = job.land_end, held + plan.block
+        shared.append(job)
+    jobs = jobs[:7] + shared + jobs[7:]
+    slots = iter(SLOTS)
+
+    def advance():
+        for k in next(slots):
+            jobs[k].step()
+
+    def plane_send(view, slots):
+        me, copies = place.plane_me, []
+        for k in range(1, place.plane):
+            t = lax.rem(me + k, place.plane)
+            copies.append(remote(view(t), slots.at[me], sends, recvs, place.plane_device(t)))
+        own = pltpu.make_async_copy(view(me), slots.at[me], local.take())
+        own.start()
+        return copies + [own]
+
     loads.x.wait()
     x = S.x
 
@@ -618,9 +748,11 @@
             x[r : r + BLOCK, lanes(at)] = (x[r : r + BLOCK, lanes(at)].astype(F32) * mask[r : r + BLOCK]).astype(BF16)
 
     columns(wide, cut)
+
     loads.wr.wait()
     S.f1[...] = dot(x[...], S.wr[...])
     local_moments(S.f1, mid, all_sums[0], False)
+    place.greeted()
     all_sums[0].start()
     stem.tables()
     all_sums[0].middle()
@@ -640,12 +772,40 @@
         spread_taps(S.tmp, tap, cells, rows, grid, store)
 
     columns(mid, hidden_one)
+    me, centre = place.plane_me, ntap // 2 * mid
+    sibling = me + 1 - 2 * lax.rem(me, 2)
+
+    def half_inputs(t):
+        start = pl.multiple_of(centre + t // 4 * lay.spatial_in, lay.spatial_in)
+        return S.col.at[:, pl.ds(start, lay.spatial_in)]
+
+    def same_core(k):
+        return lax.rem(me // 2 + k, 4) * 2 + lax.rem(me, 2)
+
+    def h1_send():
+        copies = [
+            remote(half_inputs(same_core(k)), S.h1_in.at[me], sends, recvs, place.plane_device(same_core(k)))
+            for k in range(1, 4)
+        ]
+        own = pltpu.make_async_copy(half_inputs(me), S.h1_in.at[me], local.take())
+        own.start()
+        return copies, [remote(half_inputs(me), S.h1_in.at[me], sends, recvs, place.plane_device(sibling)), own]
+
+    def h1_relay(copies):
+        more = []
+        for copy in copies:
+            copy.wait()
+        for k in range(1, 4):
+            block = S.h1_in.at[same_core(k)]
+            more.append(remote(block, block, sends, recvs, place.plane_device(sibling)))
+        return more
     loads.ws.wait()
     S.f2[...] = dot(S.col[...], S.ws[...])
     local_moments(S.f2, mid, all_sums[1], True)
     all_sums[1].start()
     stem.forward(all_sums[2], wide)
     all_sums[1].middle()
+    h1_far, h1_copies = h1_send()
     all_sums[1].finish()
 
     def hidden_two(at, j):
@@ -660,6 +820,7 @@
     local_moments(S.f3, wide, all_sums[2], False)
     all_sums[2].start()
     all_sums[2].middle()
+    h1_copies = h1_copies + h1_relay(h1_far)
     all_sums[2].finish()
 
     def branch_low(at, j):
@@ -683,6 +844,10 @@
     has_before = jnp.where(jnp.full((1, LANES), place.seg, jnp.int32) > 0, 1.0, 0.0).astype(F32)
     has_after = jnp.where(jnp.full((1, LANES), place.seg, jnp.int32) < segs - 1, 1.0, 0.0).astype(F32)
     copies = swap(S.sq, S.halo)
+    loads.stem_cot.wait()
+    stem.rear(stats[2][:, lanes(wide)], all_sums[3], wide)
+    stem_copy = pltpu.make_async_copy(S.stem_cot, R.stem_out, local.take())
+    stem_copy.start()
     for copy in copies:
         copy.wait()
 
@@ -779,16 +944,25 @@
 
     columns(wide, branch_grad)
     all_sums[3].start()
-    loads.stem_cot.wait()
-    stem.rear(stats[2][:, lanes(wide)], all_sums[4], mid)
-    stem_copy = pltpu.make_async_copy(S.stem_cot, R.stem_out, local.take())
-    stem_copy.start()
     for b in range(mid // red):
         grads[lay.squeeze : lay.squeeze + mid, lanes(b * red, red)] = dot_at(
             S.branch[:, lanes(b * mid, mid)], S.gsq[...]
         ).astype(BF16)
+    advance()
     all_sums[3].middle()
+    advance()
+    for copy in h1_copies:
+        copy.wait()
+
+    def widen(k, carry):
+        for r in blocks:
+            start = pl.multiple_of(k * rows + r, BLOCK)
+            S.h1_all[pl.ds(PAD + start, BLOCK)] = S.h1_in[k, r : r + BLOCK].astype(F32)
+        return carry
+
+    lax.fori_loop(0, place.plane, widen, 0)
     all_sums[3].finish()
+    advance()
 
     def through(k, back, src, given, dst, width):
         stat = stats[back]
@@ -824,15 +998,24 @@
         act_back(1, all_sums[4], S.f2, lambda r: S.gh[r : r + BLOCK, lanes(at)], at)
 
     columns(mid, back_two)
+    advance()
     all_sums[4].start()
     for b in range(wide // mid):
         grads[lay.expand + b * mid : lay.expand + (b + 1) * mid] = dot_at(
             S.h2[...], S.g3[:, lanes(b * mid, mid)]
         ).astype(BF16)
+    advance()
+    stem.back(stats[3][:, lanes(wide)], lay.stem)
     all_sums[4].middle()
+    advance()
     all_sums[4].finish()
+    advance()
     through(1, 4, S.f2, S.gy, S.g2, mid)
+
+    def output_quarter(ref):
+        return lambda t: ref.at[:, pl.ds(pl.multiple_of(lax.rem(t, 4) * LANES, LANES), LANES)]
     S.z[PAD : PAD + rows, :] = dot_bt(S.g2[...], S.ws[...])
+    advance()
 
     def back_one(at, j):
         act_back(
@@ -855,23 +1038,41 @@
     columns(mid, back_one)
     all_sums[5].start()
 
-    def spatial_grad(t, carry):
-        start = pl.multiple_of(t * mid, mid)
-        grads[pl.ds(pl.multiple_of(lay.spatial + start, LANES), mid)] = dot_at(
-            S.col[:, lanes(start, mid)], S.g2[...]
-        ).astype(BF16)
-        return carry
-
-    lax.fori_loop(0, ntap, spatial_grad, 0)
+    g_copies = plane_send(output_quarter(S.g2), S.g2_in)
+    advance()
     all_sums[5].middle()
-    stem.back(stats[4][:, lanes(mid)], lay.stem)
+    advance()
     all_sums[5].finish()
+    advance()
     through(0, 5, S.f1, S.gy, S.g1, mid)
     for b in range(wide // mid):
         grads[lay.reduce + b * mid : lay.reduce + (b + 1) * mid] = dot_at(
             x[:, lanes(b * mid, mid)], S.g1[...]
         ).astype(BF16)
+    advance()
+    for copy in g_copies:
+        copy.wait()
+    all_rows = place.plane * rows
+    g_all = S.g2_in[...].reshape(all_rows, LANES)
+    for t, (di, dj) in enumerate(TAPS):
+        off = PAD + di * grid + dj
+
+        def shifted(k, carry):
+            for r in range(0, rows, BLOCK):
+                start = pl.multiple_of(k * rows + r, BLOCK)
+                for at in range(0, lay.spatial_in, LANES):
+                    v = S.h1_all[pl.ds(start, BLOCK + 2 * PAD), at : at + LANES][off : off + BLOCK]
+                    v = v * tap[t, r % cells : r % cells + BLOCK]
+                    S.h1_tap[pl.ds(start, BLOCK), at : at + LANES] = v.astype(BF16)
+            return carry
+
+        lax.fori_loop(0, place.plane, shifted, 0)
+        block = dot_at(g_all, S.h1_tap[...])
+        S.shares[t * lay.spatial_in : (t + 1) * lay.spatial_in] = block.T.astype(BF16)
+        if t % 2 == 1 or t == ntap - 1:
+            advance()
     S.z[PAD : PAD + rows, lanes(0, wide)] = dot_bt(S.g1[...], S.wr[...])
+    advance()
 
     def features_grad(at, j):
         for r in blocks:
@@ -883,35 +1084,13 @@
     feat_copy = pltpu.make_async_copy(S.g3, R.grad_features, local.take())
     feat_copy.start()
 
-    jobs, land = [], 0
-    for group in job_list(lay, mid):
-        for base, size, kind in group:
-            job = Job(
-                place, grads, S.landing, R.packed, base, size, bit_order(clips, segs, kind), land, local, sends, recvs
-            )
-            land = job.land_end
-            jobs.append(job)
-    for job in jobs:
-        job.scatter_start()
-    count_steps = len(jobs[0].steps)
-    for k in range(count_steps):
-        for job in jobs:
-            job.scatter_finish()
-            if k + 1 < count_steps:
-                job.scatter_start()
-            else:
-                job.own_start()
-    for job in jobs:
-        job.own_finish()
-        job.gather_start()
-    for k in range(count_steps):
-        for job in jobs:
-            job.gather_finish()
-            if k + 1 < count_steps:
-                job.gather_start()
+    advance()
+    advance()
+    while jobs:
+        jobs = [job for job in jobs if job.step() < 4]
     small = R.sums
     at = 0
-    for k, width in ((5, mid), (4, mid + LANES), (3, wide)):
+    for k, width in ((5, mid), (4, mid), (3, wide + LANES)):
         small[:, lanes(at, width)] = stats[k][...]
         at += width
     stem_copy.wait()
@@ -963,6 +1142,7 @@
         block_out=jax.ShapeDtypeStruct((rows, wide), BF16),
         grad_features=jax.ShapeDtypeStruct((rows, wide), BF16),
         packed=jax.ShapeDtypeStruct((lay.rows, mid), BF16),
+        shared=jax.ShapeDtypeStruct((lay.share_rows, LANES), BF16),
         sums=jax.ShapeDtypeStruct((2, 2 * mid + wide + LANES), F32),
         stem_out=jax.ShapeDtypeStruct((stem_cells, channels), BF16),
     )
@@ -974,11 +1154,12 @@
             return pl.BlockSpec(memory_space=pltpu.VMEM)
         return pl.BlockSpec(memory_space=pl.ANY)
 
-    jobs = [job for group in job_list(lay, mid) for job in group]
-    land = sum(landing_rows(size, bit_order(clips, segs, kind)) for _, size, kind in jobs)
-    bits = len(bit_order(clips, segs, 0))
+    plans = [plan for group in lay.plans(clips, segs) for plan in group]
+    shared = [plan for _, _, plan in lay.shared_plans(clips, segs)]
+    land = sum(plan.landing_rows for plan in plans)
+    share_land = sum(plan.landing_rows for plan in shared)
     near, far = 2 * segs, clips // 2
-    remote_count = len(jobs) * bits * 2 + 6 * (near + far) + 8
+    remote_count = sum(plan.transfers for plan in plans + shared) + 6 * (near + far) + 48
     v = pltpu.VMEM
     scratch = dict(
         x=v((rows, wide), BF16),
@@ -1023,6 +1204,12 @@
         z=v((rows + 2 * PAD, taps * mid), F32),
         grads=v((lay.rows, mid), BF16),
         landing=v((land, mid), BF16),
+        shares=v((lay.spatial_block, LANES), BF16),
+        share_landing=v((share_land, LANES), BF16),
+        h1_in=v((8, rows, lay.spatial_in), BF16),
+        h1_all=v((8 * rows + 2 * PAD, lay.spatial_in), F32),
+        h1_tap=v((8 * rows, lay.spatial_in), BF16),
+        g2_in=v((8, rows, LANES), BF16),
         frames=v((images * count * colours, side, side), BF16),
         stem_cot=v((stem_cells, channels), BF16),
         stem_wide=v((stem_cells, LANES), F32),
@@ -1039,7 +1226,7 @@
         wt=v((192, LANES), F32),
         wd=v((144, LANES), F32),
     )
-    for k, width in enumerate((mid, mid, wide + LANES, wide, mid + LANES, mid)):
+    for k, width in enumerate((mid, mid, wide + LANES, wide + LANES, mid, mid)):
         scratch[f"near{k}"] = v((near, 2, width), F32)
         scratch[f"far{k}"] = v((far, 2, width), F32)
         scratch[f"res{k}"] = v((2, width), F32)
@@ -1066,81 +1253,176 @@
 VMEM_LIMIT = 62 << 20
 
 
-def spread_kernel(lay, mid, red, wide, packed, reduce, spatial, expand, squeeze, fine, coarse, excite, stem, held, wide_held, reads, writes):
+def spread_kernel(lay, plans, shared_plans, mid, red, wide, ins, outs, names, *refs):
+    R = SimpleNamespace(**dict(zip(ins + outs + names, refs)))
     taps = len(TAPS)
-    parts = []
-    at = 0
-    while at < lay.rows:
-        size = min(512, lay.rows - at)
-        if at < lay.expand:
-            size = {lay.excite: lay.scales - lay.excite, lay.scales: lay.squeeze - lay.scales, lay.squeeze: lay.expand - lay.squeeze}[at]
-        parts.append((at, size))
-        at += size
-    copies = []
-    for k, (at, size) in enumerate(parts):
-        copy = pltpu.make_async_copy(packed.at[pl.ds(at, size)], held.at[pl.ds(at, size)], reads.at[k])
+    copies, out = [], []
+
+    def read(src, dst):
+        copy = pltpu.make_async_copy(src, dst, R.reads.at[len(copies)])
         copy.start()
         copies.append(copy)
-    out, used = [], 0
 
     def write(src, dst):
-        copy = pltpu.make_async_copy(src, dst, writes.at[len(out)])
+        copy = pltpu.make_async_copy(src, dst, R.writes.at[len(out)])
         copy.start()
         out.append(copy)
 
-    for k, (at, size) in enumerate(parts):
+    for plan in plans:
+        here = pl.ds(plan.first, plan.rows)
+        read(R.packed.at[here], R.held.at[here])
+    for _, _, plan in shared_plans:
+        here = pl.ds(plan.first, plan.rows)
+        read(R.shared.at[here], R.shares.at[here])
+    passed = [
+        (R.block_out, R.block_held, R.out_block),
+        (R.grad_features, R.features_held, R.out_features),
+        (R.stem_out, R.stem_held, R.out_stem),
+    ]
+    for src, here, _ in passed:
+        read(src, here)
+    at = 0
+    for bias, gain in (
+        (R.bias_one, R.gain_one),
+        (R.bias_two, R.gain_two),
+        (R.bias_three, R.gain_three),
+        (R.stem_bias, R.stem_gain),
+    ):
+        width = bias.shape[1]
+        bias[...] = R.sums[0:1, at : at + width]
+        gain[...] = R.sums[1:2, at : at + width]
+        at += width
+    full = R.full
+
+    def wait_and_convert(k, plan):
         copies[k].wait()
+        count, bits_of = plan.pieces()
+
+        def convert(number, carry):
+            values = bits_of(number)
+            src = pl.multiple_of(plan.packed_at(values), 16)
+            dst = pl.multiple_of(plan.first + plan.summed_at(values), 16)
+            for r in range(0, plan.piece, 16):
+                full[pl.ds(dst + r, 16)] = R.held[pl.ds(src + r, 16)].astype(F32)
+            return carry
+
+        lax.fori_loop(0, count, convert, 0)
+
+    for k, plan in enumerate(plans[:3]):
+        wait_and_convert(k, plan)
+    for k, (_, here, dst) in enumerate(passed):
+        copies[len(plans) + len(shared_plans) + k].wait()
+        write(here, dst)
+    for b in range(wide // mid):
+        write(full.at[pl.ds(lay.excite + b * red, red)], R.excite.at[:, pl.ds(b * mid, mid)])
+    for t in range(2 * taps):
+        top, at = lay.scales + t // lay.scale_taps * red, t % lay.scale_taps * red
+        write(full.at[pl.ds(top, red), pl.ds(at, red)], (R.fine if t < taps else R.coarse).at[pl.ds(t % taps * red, red)])
+    for b in range(mid // red):
+        write(full.at[pl.ds(lay.squeeze, mid), pl.ds(b * red, red)], R.squeeze.at[pl.ds(b * mid, mid)])
+    for k, plan in enumerate(plans[3:7]):
+        wait_and_convert(3 + k, plan)
+        write(full.at[pl.ds(plan.first, mid)], R.expand.at[:, pl.ds(k * mid, mid)])
+
+    for k, (tap, count, plan) in enumerate(shared_plans):
+        copies[len(plans) + k].wait()
+        number, bits_of = plan.pieces()
 
         def convert(i, carry):
-            here = pl.ds(pl.multiple_of(at + i * 32, 32), 32)
-            wide_held[here] = held[here].astype(F32)
+            values = bits_of(i)
+            src = pl.multiple_of(plan.packed_at(values), 16)
+            row = plan.summed_at(values)
+            x, y, core = values[("clip", 1)], values[("seg", 2)], values[("seg", 1)]
+            dst = (tap + row // lay.spatial_in) * mid + x * lay.spatial_in + lax.rem(row, lay.spatial_in)
+            at = lanes(pl.multiple_of((y * 2 + core) * LANES, LANES))
+            for r in range(0, plan.piece, 16):
+                here = pl.ds(pl.multiple_of(dst + r, 16), 16)
+                R.full_spatial[here, at] = R.shares[pl.ds(src + r, 16)].astype(F32)
             return carry
 
-        lax.fori_loop(0, size // 32, convert, 0)
-        block = wide_held.at[pl.ds(at, size)]
-        if at == lay.excite:
-            for b in range(wide // mid):
-                write(wide_held.at[pl.ds(at + b * red, red)], excite.at[:, pl.ds(b * mid, mid)])
-        elif at == lay.scales:
-            for t in range(2 * taps):
-                src = wide_held.at[
-                    pl.ds(at + t // lay.scale_taps * red, red), pl.ds(t % lay.scale_taps * red, red)
-                ]
-                dst = fine if t < taps else coarse
-                write(src, dst.at[pl.ds(t % taps * red, red)])
-        elif at == lay.squeeze:
-            for b in range(mid // red):
-                write(wide_held.at[pl.ds(at, mid), pl.ds(b * red, red)], squeeze.at[pl.ds(b * mid, mid)])
-        elif at == lay.stem:
-            write(block, stem)
-        elif at < lay.spatial:
-            write(block, expand.at[:, pl.ds(at - lay.expand, size)])
-        elif at < lay.reduce:
-            write(block, spatial.at[pl.ds(at - lay.spatial, size)])
-        else:
-            write(block, reduce.at[pl.ds(at - lay.reduce, size)])
+        lax.fori_loop(0, number, convert, 0)
+        here = pl.ds(tap * mid, count * mid)
+        write(R.full_spatial.at[here], R.spatial.at[here])
+    for k, plan in enumerate(plans[7:]):
+        wait_and_convert(7 + k, plan)
+        write(full.at[pl.ds(plan.first, plan.rows)], R.reduce.at[pl.ds(plan.first - lay.reduce, plan.rows)])
+    kernel, channels = R.stem_w.shape[1], R.stem_w.shape[2]
+    colours = R.stem_w.shape[0] // kernel
+    rest = R.rows.shape[0] - LANES
+    R.rows[0:LANES] = full[lay.stem : lay.stem + LANES, lanes(0)]
+    R.rows[LANES:] = full[lay.stem : lay.stem + rest, lanes(LANES)]
+    for ki in range(kernel):
+        for c in range(colours):
+            part = R.rows[pl.ds(c * kernel * 8 + ki, kernel, stride=8), :]
+            R.stem_w[ki * colours + c] = part[:, 0:channels]
+    for t in range(taps):
+        top, at = (lay.stem + t * 16, 2 * LANES) if t < 8 else (lay.stem, 3 * LANES)
+        R.diff_w[t] = full[top : top + R.diff_w.shape[1], at : at + channels]
     for copy in out:
         copy.wait()
 
 
-def spread(packed, mid, red, wide):
+def spread(clips, segs, given, sizes):
+    mid, red, wide, kernel, colours, channels, differences = sizes
     lay = Layout(wide, mid, red)
     taps = len(TAPS)
-    shapes = [(wide, mid), (taps * mid, mid), (mid, wide), (wide, red), (taps * red, red), (taps * red, red), (red, wide), (LANES, mid)]
-    return pl.pallas_call(
-        partial(spread_kernel, lay, mid, red, wide),
-        out_shape=[jax.ShapeDtypeStruct(shape, F32) for shape in shapes],
-        in_specs=[pl.BlockSpec(memory_space=pl.ANY)],
-        out_specs=[pl.BlockSpec(memory_space=pl.ANY)] * len(shapes),
-        scratch_shapes=[
-            pltpu.VMEM((lay.rows, mid), BF16),
-            pltpu.VMEM((lay.rows, mid), F32),
-            pltpu.SemaphoreType.DMA((64,)),
-            pltpu.SemaphoreType.DMA((64,)),
-        ],
+    plans = [plan for group in lay.plans(clips, segs) for plan in group]
+    shared_plans = lay.shared_plans(clips, segs)
+
+    def f32(*shape):
+        return jax.ShapeDtypeStruct(shape, F32)
+
+    outs = dict(
+        out_block=given["block_out"],
+        out_features=given["grad_features"],
+        out_stem=given["stem_out"],
+        reduce=f32(wide, mid),
+        spatial=f32(taps * mid, mid),
+        expand=f32(mid, wide),
+        squeeze=f32(wide, red),
+        fine=f32(taps * red, red),
+        coarse=f32(taps * red, red),
+        excite=f32(red, wide),
+    )
+    outs = {name: jax.ShapeDtypeStruct(out.shape, out.dtype) for name, out in outs.items()}
+    small = dict(
+        stem_w=f32(kernel * colours, kernel, channels),
+        diff_w=f32(taps, differences, channels),
+        bias_one=f32(1, mid),
+        gain_one=f32(1, mid),
+        bias_two=f32(1, mid),
+        gain_two=f32(1, mid),
+        bias_three=f32(1, wide),
+        gain_three=f32(1, wide),
+        stem_bias=f32(1, channels),
+        stem_gain=f32(1, channels),
+    )
+    scratch = dict(
+        held=pltpu.VMEM((lay.rows, mid), BF16),
+        shares=pltpu.VMEM((lay.share_rows, LANES), BF16),
+        full=pltpu.VMEM((lay.rows, mid), F32),
+        full_spatial=pltpu.VMEM((taps * mid, mid), F32),
+        rows=pltpu.VMEM((176, LANES), F32),
+        block_held=pltpu.VMEM(given["block_out"].shape, BF16),
+        features_held=pltpu.VMEM(given["grad_features"].shape, BF16),
+        stem_held=pltpu.VMEM(given["stem_out"].shape, BF16),
+        reads=pltpu.SemaphoreType.DMA((32,)),
+        writes=pltpu.SemaphoreType.DMA((64,)),
+    )
+    here, anywhere = pl.BlockSpec(memory_space=pltpu.VMEM), pl.BlockSpec(memory_space=pl.ANY)
+    names = list(outs) + list(small)
+    results = pl.pallas_call(
+        partial(
+            spread_kernel, lay, plans, shared_plans, mid, red, wide, list(given), names, list(scratch)
+        ),
+        out_shape=list(outs.values()) + list(small.values()),
+        in_specs=[here if array.size < 1 << 15 else anywhere for array in given.values()],
+        out_specs=[anywhere] * len(outs) + [here] * len(small),
+        scratch_shapes=list(scratch.values()),
         compiler_params=pltpu.CompilerParams(vmem_limit_bytes=VMEM_LIMIT),
         name="spread",
-    )(packed)
+    )(*given.values())
+    return SimpleNamespace(**dict(zip(names, results)))
 
 
 def shards(
@@ -1174,40 +1456,37 @@
         w_squeeze, w_fine, w_coarse, w_excite,
     )
     stem = (frames, stem_cotangent, stem_weight, diff_weight, stem_gain, stem_bias)
-    block_out, grad_feats, packed, sums, stem_out = block(
+    block_out, grad_feats, packed, shared, sums, stem_out = block(
         clips, segs, features, block_cotangent, res_group, deep, stem
     )
-    g_reduce, g_spatial, g_expand, g_squeeze, g_fine, g_coarse, g_excite, g_stem = spread(packed, mid, red, wide)
     kernel, colours, channels = stem_weight.shape[0], stem_weight.shape[2], stem_weight.shape[3]
-    parts = [g_stem[:, k * LANES : k * LANES + channels] for k in range(4)]
-    g_stem_w = jnp.concatenate(parts[:2])[: colours * kernel * 8].reshape(colours, kernel, 8, channels)
-    g_stem_w = jnp.transpose(g_stem_w[:, :, :kernel], (2, 1, 0, 3))
-    g_diff_w = jnp.concatenate([parts[2], parts[3][:16]]).reshape(3, 3, 16, channels)[:, :, : diff_weight.shape[2]]
-
-    def pick(row, at, width):
-        return sums[row, at : at + width]
-
+    given = dict(
+        packed=packed, shared=shared, sums=sums, block_out=block_out, grad_features=grad_feats, stem_out=stem_out
+    )
+    sizes = (mid, red, wide, kernel, colours, channels, diff_weight.shape[2])
+    g = spread(clips, segs, given, sizes)
+    g_stem_w = jnp.transpose(g.stem_w.reshape(kernel, colours, kernel, channels), (0, 2, 1, 3))
     return (
-        stem_out.reshape(stem_cotangent.shape),
-        block_out.reshape(features.shape),
-        grad_feats.reshape(features.shape),
+        g.out_stem.reshape(stem_cotangent.shape),
+        g.out_block.reshape(features.shape),
+        g.out_features.reshape(features.shape),
         g_stem_w,
-        g_diff_w,
-        pick(1, 2 * mid, channels),
-        pick(0, 2 * mid, channels),
-        g_reduce,
-        pick(1, 0, mid),
-        pick(0, 0, mid),
-        g_spatial.reshape(w_spatial.shape),
-        pick(1, mid, mid),
-        pick(0, mid, mid),
-        g_expand,
-        pick(1, 2 * mid + LANES, wide),
-        pick(0, 2 * mid + LANES, wide),
-        g_squeeze,
-        g_fine.reshape(w_fine.shape),
-        g_coarse.reshape(w_coarse.shape),
-        g_excite,
+        g.diff_w.reshape(diff_weight.shape),
+        g.stem_gain.reshape(channels),
+        g.stem_bias.reshape(channels),
+        g.reduce,
+        g.gain_one.reshape(mid),
+        g.bias_one.reshape(mid),
+        g.spatial.reshape(w_spatial.shape),
+        g.gain_two.reshape(mid),
+        g.bias_two.reshape(mid),
+        g.expand,
+        g.gain_three.reshape(wide),
+        g.bias_three.reshape(wide),
+        g.squeeze,
+        g.fine.reshape(w_fine.shape),
+        g.coarse.reshape(w_coarse.shape),
+        g.excite,
     )
 
 

time: 232 us -> 164 us (0.71)
  Pallas kernels: 221 us -> 163 us
  local copies, waits for them, and re-layouts: 9.13 us -> 0 us
    pallas_call x1, Pallas kernels: 209 us -> 145 us  [block(): pl.pallas_call(partial(block_kernel, clips, segs, grid, names, list(scrat...]
    pallas_call x1, Pallas kernels: 11.8 us -> 18.2 us  [spread(): pl.pallas_call(partial(spread_kernel, lay, plans, shared_plans, mid, red,...]
    slice x4 -> x0, local copies, waits for them, and re-layouts: 4.46 us -> none  [the longest x2 2.75 us: pick(): return sums[row, at:at + width]]
    unnamed x10 -> x0, local copies, waits for them, and re-layouts: 3.42 us -> none
where the time goes in v2:
time: 164 us
  Pallas kernels  163 us (99%)
    pallas_call x1, Pallas kernels, block(): pl.pallas_call(partial(block_kernel, clips, segs, grid, names, list(scrat...  145 us
    pallas_call x1, Pallas kernels, spread(): pl.pallas_call(partial(spread_kernel, lay, plans, shared_plans, mid, red,...  18.2 us

profile of v2, /device:TPU:0, one launch (start us, length us, event | category | flops | bytes accessed | tf_op | source)
XLA Modules:
  0.0 164.0 jit_solution(10826093068542401210)
XLA Ops:
  0.7 144.9 %block.1 = (bf16[256,2048]{1,0:T(8,128)(2,1)}, bf16[256,2048]{1,0:T(8,128)(2,1)}, bf16[5888,512]{1,0:T(8,128)(2,1)}, bf16[18432,128]{1,0:T(8,128)(2,1)}, f32[2,3200]{1,0:T(2,128)}, /*index=5*/bf16[2304,64]{1,0:T(8,128)(2,1)}) custom-call(bf16[256,2048]{1,0:T(8,128)(2,1)} %bitcast.46, bf16[256,2048]{1,0:T(8,128)(2,1)} %bitcast.47, s32[32]{0:T(128)} %refs_2_.1, ...), custom_call_target="tpu_custom_call" | custom-call | tf_op jit(solution)/shard_map/block/pallas_call | solution.py:1239
  145.6 18.2 %spread.1 = (bf16[256,2048]{1,0:T(8,128)(2,1)}, bf16[256,2048]{1,0:T(8,128)(2,1)}, bf16[2304,64]{1,0:T(8,128)(2,1)}, f32[2048,512]{1,0:T(8,128)}, f32[4608,512]{...) custom-call(bf16[5888,512]{1,0:T(8,128)(2,1)} %get-tuple-element.46., ...), custom_call_target="tpu_custom_call" | custom-call | tf_op jit(solution)/shard_map/spread/pallas_call | solution.py:1414

commit v3 on v2

--- a/solution.py
+++ b/solution.py
@@ -34,6 +34,10 @@
         return carry
 
     lax.fori_loop(0, total // step, go, 0)
+
+
+def log2(power):
+    return power.bit_length() - 1
 
 
 def lanes(start, size=LANES):
@@ -186,13 +190,18 @@
         self.landing_rows = sum(size for _, size, _ in self.sums)
         self.transfers = len(self.sums) + len(self.places)
 
-    def pieces(self):
+    def each_piece(self, body):
         bits = [bit for bit, _ in self.places]
-
-        def bits_of(number):
-            return {bit: lax.rem(lax.shift_right_logical(number, k), 2) for k, bit in enumerate(bits)}
-
-        return 1 << len(bits), bits_of
+        outer, inner = bits[:-3], bits[-3:]
+
+        def some(number, carry):
+            values = {bit: lax.rem(number // (1 << k), 2) for k, bit in enumerate(outer)}
+            for n in range(1 << len(inner)):
+                values.update({bit: (n >> k) % 2 for k, bit in enumerate(inner)})
+                body(values)
+            return carry
+
+        lax.fori_loop(0, 1 << len(outer), some, 0)
 
     def packed_at(self, values):
         return sum((values[bit] * size for bit, size in self.places), self.first)
@@ -369,7 +378,7 @@
         taps[...] = jnp.zeros(taps.shape, F32)
         row = lax.broadcasted_iota(jnp.int32, (taps.shape[1], self.band), 0)
         lane = lax.broadcasted_iota(jnp.int32, (taps.shape[1], self.band), 1)
-        place = jnp.where(row == lax.rem(lane, 8) * 64 + lane // 8, 1.0, 0.0).astype(BF16)
+        place = jnp.where(row == (lane & 7) * 64 + (lane >> 3), 1.0, 0.0).astype(BF16)
         for c in range(self.COLOURS):
             for img in range(images):
                 plane = frames[(img * 5 + 2) * self.COLOURS + c].astype(F32)
@@ -384,8 +393,8 @@
             xx[:, lanes(c * self.band, self.band)] = dot(taps[...].astype(BF16), place).astype(BF16)
         row = lax.broadcasted_iota(jnp.int32, (side, self.spread), 0)
         lane = lax.broadcasted_iota(jnp.int32, (side, self.spread), 1)
-        inside = row // 4 == lane // 16
-        channel = lax.rem(lane, 16)
+        inside = (row >> 2) == (lane >> 4)
+        channel = lane & 15
         total = None
         for f in range(5):
             for c in range(self.COLOURS):
@@ -541,8 +550,7 @@
         def plan(first, end, letters, nest):
             return Plan(clips, segs, first, end - first, letters, nest)
 
-        cut = self.expand // 512 * 512
-        bounds = [0, cut - 512, cut, self.expand]
+        bounds = list(range(0, self.expand, 512)) + [self.expand]
         early = [plan(bounds[k], bounds[k + 1], *orders) for k, orders in enumerate(EARLY)]
         middle = [
             plan(self.expand + k * quarter, self.expand + (k + 1) * quarter, *orders)
@@ -561,31 +569,34 @@
         return parts
 
 
-EARLY = (("cxypq", "cxypq"), ("cpyxq", "cyxpq"), ("cyxpq", "cpxqy"))
-MIDDLE = (("cpxqy", "cpyxq"), ("cpxyq", "cpxqy"), ("cpqyx", "cxypq"), ("cxypq", "cxpyq"))
-SPATIAL = ("cxypq", "cypqx", "cyxpq", "cpxqy", "cpqyx")
-LATE = (("cyxpq", "cyxpq"), ("cyxpq", "cxpqy"))
+EARLY = (("cpqyx", "cyxpq"), ("cypqx", "cyxpq"), ("cyxpq", "cxpqy"), ("cyxpq", "cxypq"))
+MIDDLE = (("cypxq", "cyxpq"), ("cxpqy", "cypxq"), ("cpyxq", "cpyxq"), ("cpyxq", "cxpqy"))
+SPATIAL = ("cxypq", "cyxpq", "cypxq", "cpxyq", "cpqxy")
+LATE = (("cxypq", "cxpqy"), ("cyxpq", "cyxpq"))
 SLOTS = (
     (0, 1),
-    (0, 1),
+    (0, 1, 2),
+    (2, 0, 1),
     (),
     (),
-    (3, 4, 5, 6, 1),
-    (3, 4, 5, 6, 0, 1, 2),
+    (),
+    (4, 5, 6, 7, 1, 2),
+    (3, 0),
+    (4, 5, 6, 7, 3, 1, 2),
+    (0,),
     (),
     (),
-    (3, 2),
-    (4, 6, 0, 1),
-    (5,),
-    (12, 13, 0),
-    (7, 3, 1, 2),
-    (12, 13, 8, 4, 5, 6, 0, 1, 2),
-    (7, 9, 3, 0),
-    (8, 10, 6, 1, 2),
-    (7, 9, 11),
-    (12, 7, 0),
-    (8, 10, 6, 1),
-    (8, 2, 6, 13, 11, 4, 12, 9, 2, 3, 7, 0, 1, 9, 3, 5, 8, 10, 2, 6, 10, 12, 11, 13, 4, 5, 7, 2, 0, 4, 5, 11, 9, 3, 1, 6, 13, 10, 8, 1, 2, 12, 5, 7, 9, 12, 4, 0, 2, 11, 6, 3, 13, 0, 11, 13, 3, 10, 8, 5, 13, 7, 12, 4, 9, 7, 3, 11, 6, 8, 3, 12, 5, 13, 10, 6, 8, 4, 11, 12, 11, 13, 9, 5, 9, 5, 10, 12, 13, 4, 10, 12, 13, 4),
+    (3, 4, 0, 5, 6, 7, 1, 2, 0),
+    (),
+    (4, 13, 1, 14),
+    (3, 8, 5, 6, 2),
+    (4, 13, 9, 0, 7, 1, 2, 14),
+    (3, 8, 10, 5, 6, 2),
+    (4, 9, 0, 11, 1),
+    (3, 4, 8, 10, 12),
+    (3, 13, 8, 0, 5, 6, 7, 11, 1, 2, 14),
+    (),
+    (3, 4, 9, 10, 5, 13, 8, 9, 10, 6, 7, 12, 4, 2, 11, 7, 0, 5, 14, 13, 11, 8, 0, 4, 1, 3, 7, 9, 10, 2, 1, 6, 5, 14, 12, 8, 3, 2, 13, 12, 10, 9, 11, 13, 3, 4, 6, 5, 7, 12, 14, 4, 11, 14, 13, 10, 6, 8, 7, 14, 5, 9, 8, 12, 13, 5, 6, 11, 14, 6, 10, 7, 12, 13, 10, 7, 14, 9, 11, 9, 13, 12, 11, 14, 13, 12, 14),
 )
 
 
@@ -610,19 +621,20 @@
         copy.start()
         return copy
 
-    loads = SimpleNamespace(
-        x=load(R.x, S.x),
-        frames=load(R.frames, S.frames),
-        wr=load(R.wr, S.wr),
-        ws=load(R.ws, S.ws),
-        we=load(R.we, S.we),
-        wq=load(R.wq, S.wq),
-        wf=load(R.wf, wfine),
-        wc=load(R.wc, wcoarse),
-        wx=load(R.wx, S.wx),
-        cot=load(R.cot, S.cot),
-        stem_cot=load(R.stem_cot, S.stem_cot),
-    )
+    x_load, wr_load = load(R.x, S.x), load(R.wr, S.wr)
+
+    def other_loads():
+        return SimpleNamespace(
+            frames=load(R.frames, S.frames),
+            ws=load(R.ws, S.ws),
+            we=load(R.we, S.we),
+            wq=load(R.wq, S.wq),
+            wf=load(R.wf, wfine),
+            wc=load(R.wc, wcoarse),
+            wx=load(R.wx, S.wx),
+            cot=load(R.cot, S.cot),
+            stem_cot=load(R.stem_cot, S.stem_cot),
+        )
 
     place.greet()
 
@@ -636,33 +648,39 @@
         side = side_of(groups[k])
         return acc + side * side
 
-    count = lax.fori_loop(0, total_groups, area, jnp.int32(0)) * segs
-    inv = 1.0 / jnp.full((1, LANES), count.astype(F32), F32)
     cell = lax.broadcasted_iota(jnp.int32, (cells, LANES), 0)
-    ci, cj = cell // grid, lax.rem(cell, grid)
+    ci, cj = cell >> log2(grid), cell & (grid - 1)
     for img in range(images):
         side = side_of(groups[place.clip * images + img])
         S.mask[img * cells : (img + 1) * cells] = jnp.where((ci < side) & (cj < side), 1.0, 0.0).astype(F32)
     half = grid // 2
-    small = lax.rem(cell, half * half)
-    si, sj = small // half, lax.rem(small, half)
-    for t, (di, dj) in enumerate(TAPS):
-        ok = (ci + di >= 0) & (ci + di < grid) & (cj + dj >= 0) & (cj + dj < grid)
-        S.tap[t] = jnp.where(ok, 1.0, 0.0).astype(F32)
-        ok = (si + di >= 0) & (si + di < half) & (sj + dj >= 0) & (sj + dj < half)
-        S.tap_small[t] = jnp.where(ok, 1.0, 0.0).astype(F32)
     mask, tap, tap_small = S.mask, S.tap, S.tap_small
-    srow = lax.broadcasted_iota(jnp.int32, (images * half * half, rows), 0)
-    brow = lax.broadcasted_iota(jnp.int32, (images * half * half, rows), 1)
-    parent = (brow // cells) * half * half + (lax.rem(brow, cells) // grid) // 2 * half + lax.rem(brow, grid) // 2
-    S.pool[...] = jnp.where(srow == parent, 0.25, 0.0).astype(BF16)
-    brow = lax.broadcasted_iota(jnp.int32, (rows, images * half * half), 0)
-    srow = lax.broadcasted_iota(jnp.int32, (rows, images * half * half), 1)
-    parent = (brow // cells) * half * half + (lax.rem(brow, cells) // grid) // 2 * half + lax.rem(brow, grid) // 2
-    S.up[...] = jnp.where(srow == parent, 1.0, 0.0).astype(BF16)
-    for ref in (S.tmp, S.z, S.tmp_small, S.h1_all):
-        ref[:PAD] = jnp.zeros((PAD, ref.shape[1]), F32)
-        ref[ref.shape[0] - PAD :] = jnp.zeros((PAD, ref.shape[1]), F32)
+
+    def parent_of(row):
+        i, j = (row & (cells - 1)) >> log2(grid), row & (grid - 1)
+        return (row >> log2(cells)) * half * half + (i >> 1) * half + (j >> 1)
+
+    def prepare():
+        small = cell & (half * half - 1)
+        si, sj = small >> log2(half), small & (half - 1)
+        for t, (di, dj) in enumerate(TAPS):
+            ok = (ci + di >= 0) & (ci + di < grid) & (cj + dj >= 0) & (cj + dj < grid)
+            tap[t] = jnp.where(ok, 1.0, 0.0).astype(F32)
+            ok = (si + di >= 0) & (si + di < half) & (sj + dj >= 0) & (sj + dj < half)
+            tap_small[t] = jnp.where(ok, 1.0, 0.0).astype(F32)
+        shape = (images * half * half, rows)
+        here = lax.broadcasted_iota(jnp.int32, shape, 0) == parent_of(lax.broadcasted_iota(jnp.int32, shape, 1))
+        S.pool[...] = jnp.where(here, 0.25, 0.0).astype(BF16)
+        here = lax.broadcasted_iota(jnp.int32, shape[::-1], 1) == parent_of(
+            lax.broadcasted_iota(jnp.int32, shape[::-1], 0)
+        )
+        S.up[...] = jnp.where(here, 1.0, 0.0).astype(BF16)
+        for ref in (S.tmp, S.z, S.tmp_small, S.h1_all):
+            ref[:PAD] = jnp.zeros((PAD, ref.shape[1]), F32)
+            ref[ref.shape[0] - PAD :] = jnp.zeros((PAD, ref.shape[1]), F32)
+        count = lax.fori_loop(0, total_groups, area, jnp.int32(0)) * segs
+        return 1.0 / jnp.full((1, LANES), count.astype(F32), F32)
+
     grads = S.grads
 
     near = [S.near0, S.near1, S.near2, S.near3, S.near4, S.near5]
@@ -724,7 +742,7 @@
         job = Job(place, plan, (S.shares, S.share_landing, R.shared), held, land, sems)
         land, held = job.land_end, held + plan.block
         shared.append(job)
-    jobs = jobs[:7] + shared + jobs[7:]
+    jobs = jobs[:8] + shared + jobs[8:]
     slots = iter(SLOTS)
 
     def advance():
@@ -740,7 +758,7 @@
         own.start()
         return copies + [own]
 
-    loads.x.wait()
+    x_load.wait()
     x = S.x
 
     def cut(at, j):
@@ -749,11 +767,13 @@
 
     columns(wide, cut)
 
-    loads.wr.wait()
+    wr_load.wait()
     S.f1[...] = dot(x[...], S.wr[...])
     local_moments(S.f1, mid, all_sums[0], False)
     place.greeted()
     all_sums[0].start()
+    loads = other_loads()
+    inv = prepare()
     stem.tables()
     all_sums[0].middle()
     loads.frames.wait()
@@ -924,6 +944,7 @@
         grads[top : top + red, lanes(t % lay.scale_taps * red, red)] = dot_at(
             S.cc[:, lanes(t * red, red)], S.gm[...]
         ).astype(BF16)
+    advance()
     for copy in copies:
         copy.wait()
     for r in blocks:
@@ -992,6 +1013,7 @@
         ar.put(1, at, total_of(q))
 
     through(2, 3, S.f3, S.gb, S.g3, wide)
+    advance()
     S.gh[...] = dot_bt(S.g3[...], S.we[...])
 
     def back_two(at, j):
@@ -1006,6 +1028,7 @@
         ).astype(BF16)
     advance()
     stem.back(stats[3][:, lanes(wide)], lay.stem)
+    advance()
     all_sums[4].middle()
     advance()
     all_sums[4].finish()
@@ -1253,27 +1276,39 @@
 VMEM_LIMIT = 62 << 20
 
 
+AHEAD = 16
+
+
 def spread_kernel(lay, plans, shared_plans, mid, red, wide, ins, outs, names, *refs):
     R = SimpleNamespace(**dict(zip(ins + outs + names, refs)))
     taps = len(TAPS)
     copies, out = [], []
 
     def read(src, dst):
-        copy = pltpu.make_async_copy(src, dst, R.reads.at[len(copies)])
-        copy.start()
-        copies.append(copy)
+        copies.append(pltpu.make_async_copy(src, dst, R.reads.at[len(copies)]))
+
+    arrived = iter(range(len(plans) + len(shared_plans) + 3))
+
+    def arrive():
+        k = next(arrived)
+        if k == 0:
+            for copy in copies[:AHEAD]:
+                copy.start()
+        copies[k].wait()
+        if k + AHEAD < len(copies):
+            copies[k + AHEAD].start()
 
     def write(src, dst):
         copy = pltpu.make_async_copy(src, dst, R.writes.at[len(out)])
         copy.start()
         out.append(copy)
 
-    for plan in plans:
+    for plan in plans[:8] + [plan for _, _, plan in shared_plans] + plans[8:]:
         here = pl.ds(plan.first, plan.rows)
-        read(R.packed.at[here], R.held.at[here])
-    for _, _, plan in shared_plans:
-        here = pl.ds(plan.first, plan.rows)
-        read(R.shared.at[here], R.shares.at[here])
+        if plan in plans:
+            read(R.packed.at[here], R.held.at[here])
+        else:
+            read(R.shared.at[here], R.shares.at[here])
     passed = [
         (R.block_out, R.block_held, R.out_block),
         (R.grad_features, R.features_held, R.out_features),
@@ -1294,25 +1329,20 @@
         at += width
     full = R.full
 
-    def wait_and_convert(k, plan):
-        copies[k].wait()
-        count, bits_of = plan.pieces()
-
-        def convert(number, carry):
-            values = bits_of(number)
-            src = pl.multiple_of(plan.packed_at(values), 16)
-            dst = pl.multiple_of(plan.first + plan.summed_at(values), 16)
+    def wait_and_convert(plan):
+        arrive()
+
+        def convert(values):
+            src = plan.packed_at(values)
+            dst = plan.first + plan.summed_at(values)
             for r in range(0, plan.piece, 16):
-                full[pl.ds(dst + r, 16)] = R.held[pl.ds(src + r, 16)].astype(F32)
-            return carry
-
-        lax.fori_loop(0, count, convert, 0)
-
-    for k, plan in enumerate(plans[:3]):
-        wait_and_convert(k, plan)
-    for k, (_, here, dst) in enumerate(passed):
-        copies[len(plans) + len(shared_plans) + k].wait()
-        write(here, dst)
+                here = pl.ds(pl.multiple_of(dst + r, 16), 16)
+                full[here] = R.held[pl.ds(pl.multiple_of(src + r, 16), 16)].astype(F32)
+
+        plan.each_piece(convert)
+
+    for plan in plans[:4]:
+        wait_and_convert(plan)
     for b in range(wide // mid):
         write(full.at[pl.ds(lay.excite + b * red, red)], R.excite.at[:, pl.ds(b * mid, mid)])
     for t in range(2 * taps):
@@ -1320,32 +1350,31 @@
         write(full.at[pl.ds(top, red), pl.ds(at, red)], (R.fine if t < taps else R.coarse).at[pl.ds(t % taps * red, red)])
     for b in range(mid // red):
         write(full.at[pl.ds(lay.squeeze, mid), pl.ds(b * red, red)], R.squeeze.at[pl.ds(b * mid, mid)])
-    for k, plan in enumerate(plans[3:7]):
-        wait_and_convert(3 + k, plan)
+    for k, plan in enumerate(plans[4:8]):
+        wait_and_convert(plan)
         write(full.at[pl.ds(plan.first, mid)], R.expand.at[:, pl.ds(k * mid, mid)])
 
-    for k, (tap, count, plan) in enumerate(shared_plans):
-        copies[len(plans) + k].wait()
-        number, bits_of = plan.pieces()
-
-        def convert(i, carry):
-            values = bits_of(i)
-            src = pl.multiple_of(plan.packed_at(values), 16)
-            row = plan.summed_at(values)
+    for tap, count, plan in shared_plans:
+        arrive()
+
+        def convert(values):
+            src, row = plan.packed_at(values), plan.summed_at(values)
             x, y, core = values[("clip", 1)], values[("seg", 2)], values[("seg", 1)]
-            dst = (tap + row // lay.spatial_in) * mid + x * lay.spatial_in + lax.rem(row, lay.spatial_in)
+            dst = (tap + row // lay.spatial_in) * mid + x * lay.spatial_in + row % lay.spatial_in
             at = lanes(pl.multiple_of((y * 2 + core) * LANES, LANES))
             for r in range(0, plan.piece, 16):
                 here = pl.ds(pl.multiple_of(dst + r, 16), 16)
-                R.full_spatial[here, at] = R.shares[pl.ds(src + r, 16)].astype(F32)
-            return carry
-
-        lax.fori_loop(0, number, convert, 0)
+                R.full_spatial[here, at] = R.shares[pl.ds(pl.multiple_of(src + r, 16), 16)].astype(F32)
+
+        plan.each_piece(convert)
         here = pl.ds(tap * mid, count * mid)
         write(R.full_spatial.at[here], R.spatial.at[here])
-    for k, plan in enumerate(plans[7:]):
-        wait_and_convert(7 + k, plan)
+    for plan in plans[8:]:
+        wait_and_convert(plan)
         write(full.at[pl.ds(plan.first, plan.rows)], R.reduce.at[pl.ds(plan.first - lay.reduce, plan.rows)])
+    for _, here, dst in passed:
+        arrive()
+        write(here, dst)
     kernel, channels = R.stem_w.shape[1], R.stem_w.shape[2]
     colours = R.stem_w.shape[0] // kernel
     rest = R.rows.shape[0] - LANES

time: 164 us -> 157 us (0.957)
  Pallas kernels: 163 us -> 156 us
    pallas_call x1, Pallas kernels: 18.2 us -> 14 us  [spread(): pl.pallas_call(partial(spread_kernel, lay, plans, shared_plans, mid, red,...]
    pallas_call x1, Pallas kernels: 145 us -> 142 us  [block(): pl.pallas_call(partial(block_kernel, clips, segs, grid, names, list(scrat...]
where the time goes in v3:
time: 157 us
  Pallas kernels  156 us (99%)
    pallas_call x1, Pallas kernels, block(): pl.pallas_call(partial(block_kernel, clips, segs, grid, names, list(scrat...  142 us
    pallas_call x1, Pallas kernels, spread(): pl.pallas_call(partial(spread_kernel, lay, plans, shared_plans, mid, red,...  14 us

profile of v3, /device:TPU:0, one launch (start us, length us, event | category | flops | bytes accessed | tf_op | source)
XLA Modules:
  0.0 156.8 jit_solution(6400243807638748956)
XLA Ops:
  0.7 142.0 %block.1 = (bf16[256,2048]{1,0:T(8,128)(2,1)}, bf16[256,2048]{1,0:T(8,128)(2,1)}, bf16[5888,512]{1,0:T(8,128)(2,1)}, bf16[18432,128]{1,0:T(8,128)(2,1)}, f32[2,3200]{1,0:T(2,128)}, /*index=5*/bf16[2304,64]{1,0:T(8,128)(2,1)}) custom-call(bf16[256,2048]{1,0:T(8,128)(2,1)} %bitcast.46, bf16[256,2048]{1,0:T(8,128)(2,1)} %bitcast.47, s32[32]{0:T(128)} %refs_2_.1, ...), custom_call_target="tpu_custom_call" | custom-call | tf_op jit(solution)/shard_map/block/pallas_call | solution.py:1262
  142.6 14.0 %spread.1 = (bf16[256,2048]{1,0:T(8,128)(2,1)}, bf16[256,2048]{1,0:T(8,128)(2,1)}, bf16[2304,64]{1,0:T(8,128)(2,1)}, f32[2048,512]{1,0:T(8,128)}, f32[4608,512]{...) custom-call(bf16[5888,512]{1,0:T(8,128)(2,1)} %get-tuple-element.46., ...), custom_call_target="tpu_custom_call" | custom-call | tf_op jit(solution)/shard_map/spread/pallas_call | solution.py:1443

commit v4 on v3

--- a/solution.py
+++ b/solution.py
@@ -146,16 +146,20 @@
         self.copies = self._send(self.near_buf, p.near_me, p.near, p.near_device)
 
     def middle(self):
-        p = self.place
-        for copy in self.copies:
-            copy.wait()
+        p, sent = self.place, self.copies
+        for copy in sent:
+            copy.wait_recv()
         self.far_buf[p.far_me] = self._add(self.near_buf, p.near)
         self.copies = self._send(self.far_buf, p.far_me, p.far, p.far_device)
+        for copy in sent:
+            copy.wait_send()
 
     def finish(self):
         for copy in self.copies:
-            copy.wait()
+            copy.wait_recv()
         self.result[...] = self._add(self.far_buf, self.place.far)
+        for copy in self.copies:
+            copy.wait_send()
 
 
 def bit_order(clips, segs, letters):
@@ -221,7 +225,7 @@
             if halved:
                 away = held + (1 - bit) * size
                 held = held + bit * size
-            self.sums.append((held, away, size, device, land))
+            self.sums.append((held, away, size, halved, device, land))
             land += size
         self.held, self.piece, self.land_end = held, plan.piece, land
         first = plan.first
@@ -238,14 +242,17 @@
         return ref.at[pl.ds(start, size)]
 
     def scatter_start(self):
-        held, away, size, device, land = self.sums[self.at]
+        held, away, size, halved, device, land = self.sums[self.at]
         self.copy = remote(
             self._rows(self.grads, away, size), self._rows(self.landing, land, size), self.sends, self.recvs, device
         )
 
     def scatter_finish(self):
-        held, away, size, device, land = self.sums[self.at]
-        self.copy.wait()
+        held, away, size, halved, device, land = self.sums[self.at]
+        sent = self.copy
+        sent.wait_recv()
+        if not halved:
+            sent.wait_send()
         block = 32 if size % 32 == 0 else 16
 
         def add(k, carry):
@@ -256,46 +263,48 @@
 
         lax.fori_loop(0, size // block, add, 0)
         self.at += 1
+        return [sent] if halved else []
 
     def own_start(self):
-        self.copy = pltpu.make_async_copy(
-            self._rows(self.grads, self.held, self.piece),
-            self._rows(self.packed, self.first, self.piece),
-            self.local.take(),
-        )
-        self.copy.start()
+        mine = self._rows(self.grads, self.held, self.piece)
+        self.own = pltpu.make_async_copy(mine, self._rows(self.packed, self.first, self.piece), self.local.take())
+        self.own.start()
         self.at = len(self.places)
-
-    def gather_start(self):
+        self.gather_start(mine)
+
+    def gather_start(self, src=None):
         first, size, device = self.places[self.at - 1]
         mine = self._rows(self.packed, first, size)
-        self.copy = remote(mine, mine, self.sends, self.recvs, device)
+        self.copy = remote(mine if src is None else src, mine, self.sends, self.recvs, device)
 
     def gather_finish(self):
         self.at -= 1
-        self.copy.wait()
+        sent = self.copy
+        sent.wait_recv()
+        if self.at == len(self.places) - 1:
+            self.own.wait()
+        return [sent]
 
     def step(self):
+        sent = []
         if self.phase == 0:
             self.scatter_start()
             self.phase = 1
         elif self.phase == 1:
-            self.scatter_finish()
+            sent = self.scatter_finish()
             if self.at < len(self.sums):
                 self.scatter_start()
             else:
                 self.own_start()
                 self.phase = 2
         elif self.phase == 2:
-            self.copy.wait()
-            self.gather_start()
-            self.phase = 3
-        elif self.phase == 3:
-            self.gather_finish()
+            sent = self.gather_finish()
             if self.at > 0:
                 self.gather_start()
             else:
-                self.phase = 4
+                self.phase = 3
+        for copy in sent:
+            copy.wait_send()
         return self.phase
 
 
@@ -569,34 +578,34 @@
         return parts
 
 
-EARLY = (("cpqyx", "cyxpq"), ("cypqx", "cyxpq"), ("cyxpq", "cxpqy"), ("cyxpq", "cxypq"))
-MIDDLE = (("cypxq", "cyxpq"), ("cxpqy", "cypxq"), ("cpyxq", "cpyxq"), ("cpyxq", "cxpqy"))
-SPATIAL = ("cxypq", "cyxpq", "cypxq", "cpxyq", "cpqxy")
-LATE = (("cxypq", "cxpqy"), ("cyxpq", "cyxpq"))
+EARLY = (("cypxq", "cxypq"), ("cpqyx", "cyxpq"), ("cxypq", "cyxpq"), ("cyxpq", "cpxqy"))
+MIDDLE = (("cyxpq", "cyxpq"), ("cpyqx", "cxypq"), ("cpyxq", "cxpqy"), ("cxpqy", "cyxpq"))
+SPATIAL = ("cpxyq", "cyxpq", "cyxpq", "cyxpq", "cxpyq")
+LATE = (("cyxpq", "cpyqx"), ("cyxpq", "cxpqy"))
 SLOTS = (
-    (0, 1),
-    (0, 1, 2),
-    (2, 0, 1),
+    (1, 0),
+    (2, 1, 0, 2),
+    (1, 0, 2),
     (),
     (),
     (),
-    (4, 5, 6, 7, 1, 2),
-    (3, 0),
-    (4, 5, 6, 7, 3, 1, 2),
-    (0,),
+    (2, 6, 7, 1, 0, 4, 5),
+    (),
+    (6, 7, 3, 4, 5, 2, 1, 3, 0),
     (),
     (),
-    (3, 4, 0, 5, 6, 7, 1, 2, 0),
+    (6, 7, 1, 4, 3, 5, 2),
+    (0, 7, 1, 2),
     (),
-    (4, 13, 1, 14),
-    (3, 8, 5, 6, 2),
-    (4, 13, 9, 0, 7, 1, 2, 14),
-    (3, 8, 10, 5, 6, 2),
-    (4, 9, 0, 11, 1),
-    (3, 4, 8, 10, 12),
-    (3, 13, 8, 0, 5, 6, 7, 11, 1, 2, 14),
+    (7, 13, 0, 14),
+    (2, 6, 1, 3, 13, 4, 5, 14, 8),
+    (2, 7, 9, 3, 0, 4),
+    (6, 1, 10, 5, 8),
     (),
-    (3, 4, 9, 10, 5, 13, 8, 9, 10, 6, 7, 12, 4, 2, 11, 7, 0, 5, 14, 13, 11, 8, 0, 4, 1, 3, 7, 9, 10, 2, 1, 6, 5, 14, 12, 8, 3, 2, 13, 12, 10, 9, 11, 13, 3, 4, 6, 5, 7, 12, 14, 4, 11, 14, 13, 10, 6, 8, 7, 14, 5, 9, 8, 12, 13, 5, 6, 11, 14, 6, 10, 7, 12, 13, 10, 7, 14, 9, 11, 9, 13, 12, 11, 14, 13, 12, 14),
+    (7, 9, 3, 12, 13, 11, 4, 5),
+    (),
+    (6, 7, 10, 8),
+    (9, 12, 14, 13, 11, 4, 5, 7, 10, 2, 0, 2, 13, 8, 14, 9, 12, 4, 5, 1, 3, 11, 6, 1, 10, 14, 0, 13, 7, 4, 9, 0, 3, 12, 7, 8, 11, 5, 13, 10, 6, 14, 4, 9, 3, 12, 11, 4, 3, 14, 8, 13, 6, 12, 5, 5, 14, 9, 10, 9, 13, 11, 8, 6, 8, 14, 6, 10, 12, 10, 12, 13, 11, 13, 14, 11, 14),
 )
 
 
@@ -1110,7 +1119,7 @@
     advance()
     advance()
     while jobs:
-        jobs = [job for job in jobs if job.step() < 4]
+        jobs = [job for job in jobs if job.step() < 3]
     small = R.sums
     at = 0
     for k, width in ((5, mid), (4, mid), (3, wide + LANES)):

time: 157 us -> 156 us (level)
  no operation moved by 1% of the time
where the time goes in v4:
time: 156 us
  Pallas kernels  155 us (99%)
    pallas_call x1, Pallas kernels, block(): pl.pallas_call(partial(block_kernel, clips, segs, grid, names, list(scrat...  141 us
    pallas_call x1, Pallas kernels, spread(): pl.pallas_call(partial(spread_kernel, lay, plans, shared_plans, mid, red,...  14 us

profile of v4, /device:TPU:0, one launch (start us, length us, event | category | flops | bytes accessed | tf_op | source)
XLA Modules:
  0.0 156.1 jit_solution(8002566052676156379)
XLA Ops:
  0.7 141.2 %block.1 = (bf16[256,2048]{1,0:T(8,128)(2,1)}, bf16[256,2048]{1,0:T(8,128)(2,1)}, bf16[5888,512]{1,0:T(8,128)(2,1)}, bf16[18432,128]{1,0:T(8,128)(2,1)}, f32[2,3200]{1,0:T(2,128)}, /*index=5*/bf16[2304,64]{1,0:T(8,128)(2,1)}) custom-call(bf16[256,2048]{1,0:T(8,128)(2,1)} %bitcast.46, bf16[256,2048]{1,0:T(8,128)(2,1)} %bitcast.47, s32[32]{0:T(128)} %refs_2_.1, ...), custom_call_target="tpu_custom_call" | custom-call | tf_op jit(solution)/shard_map/block/pallas_call | solution.py:1271
  141.9 14.0 %spread.1 = (bf16[256,2048]{1,0:T(8,128)(2,1)}, bf16[256,2048]{1,0:T(8,128)(2,1)}, bf16[2304,64]{1,0:T(8,128)(2,1)}, f32[2048,512]{1,0:T(8,128)}, f32[4608,512]{...) custom-call(bf16[5888,512]{1,0:T(8,128)(2,1)} %get-tuple-element.46., ...), custom_call_target="tpu_custom_call" | custom-call | tf_op jit(solution)/shard_map/spread/pallas_call | solution.py:1452
